TPU v7x, 128 devices: a whole 4x4x4 slice. The times are simulated.
128 devices in a mesh: sub: 32 (over y, x, core), grp: 4 (over z).
Axes of the slice: x: 4, y: 4, z: 4, core: 2. Of those that a mesh axis runs over, the one named last changes fastest.
Arguments:
- inverse_blocks: bfloat16 [128, 2304, 2304], P(('sub', 'grp'))
- primal_loads: bfloat16 [128, 2304, 128], P(('sub', 'grp'))
- mortar_values: bfloat16 [128, 768, 768], P(('sub', 'grp')), may hold values from -1.5 to 1.5
- segment_ids: int32 [128, 768], P(('sub', 'grp')), may hold values from 0 to 47, never falling along the last dimension, each value on 1 to 32 neighbouring positions
- slave_weights: float32 [128, 768], P(('sub', 'grp')), may hold values from 0.5 to 2
- rigid_modes: float32 [128, 6, 1536], P(('sub', 'grp')), may hold values from -6 to 6
- coarse_inverse: float32 [768, 768], P(('sub', 'grp')), as said below
- candidates: int32 [128, 384], P(('sub', 'grp')), may hold values from 0 to 767, as said below
- start_multipliers: float32 [128, 768, 128], P(('sub', 'grp')), may hold values from -6 to 6
Outputs:
- multipliers: float32 [128, 768, 128], P(('sub', 'grp'))
- gradient: float32 [128, 768, 128], P(('sub', 'grp'))
Inputs may be any that keep to these rules, and one draw needn't show every extreme that they name: `segment_ids`: along each row the block numbers never fall, and each block has 1 to 32 multipliers. The candidates of one subdomain are distinct. coarse_inverse is symmetric.
All inputs are finite; a program needn't handle non-finite values.
Results may differ from a plain program's by a relative error of at most 0.0075.
Values may be sent and summed in bfloat16 or wider, within the bound.
No kernel may reach another device: no remote copies, remote signals or barrier semaphores. Data moves between devices by JAX's collectives and lax.ppermute only.
A program may use at most 64 MiB of HBM per device.

v0:
```python
import functools

import jax
import jax.numpy as jnp
import numpy as np
from jax import lax
from jax.experimental import pallas as pl
from jax.experimental.pallas import tpu as pltpu
from jax.sharding import PartitionSpec as P

STEPS = 3
AXES = ("sub", "grp")
F32, BF16 = jnp.float32, jnp.bfloat16
TILE = 128
TILE_ROWS = 192
HALO = 32
MIB = 1 << 20


def shifted(block, distance):
    size = lax.axis_size("sub")
    return lax.ppermute(block, "sub", [((i - distance) % size, i) for i in range(size)])


def swapped(block):
    size = lax.axis_size("sub")
    return lax.ppermute(block, "sub", [(i ^ 1, i) for i in range(size)])


def swapped_out(block):
    size = lax.axis_size("sub")
    other = [(i + 1 if i % 2 else i - 1) % size for i in range(size)]
    return lax.ppermute(block, "sub", [(other[i], i) for i in range(size)])


def is_odd():
    return lax.rem(lax.axis_index("sub"), 2) == 1


def rows_of(flat, count):
    width = flat.shape[1] // count
    return jnp.concatenate([flat[:, width * k : width * (k + 1)] for k in range(count)], axis=0)


def dot(left, right):
    return jnp.dot(left, right, preferred_element_type=F32)


def halves(value):
    high = value.astype(BF16).astype(F32)
    return high, (value - high).astype(BF16).astype(F32)


def column(row):
    return jnp.broadcast_to(row, (TILE, row.shape[1])).T


def mortar_times(tiles, values):
    count = values.shape[0] // TILE
    rows = TILE + 2 * HALO
    parts = [
        dot(tiles[rows * t : rows * (t + 1), :], values[TILE * t : TILE * (t + 1)])
        for t in range(count)
    ]
    out = []
    none = jnp.zeros((HALO, values.shape[1]), F32)
    for t in range(count):
        before = parts[t - 1][TILE + HALO :] if t else none
        after = parts[t + 1][TILE : TILE + HALO] if t + 1 < count else none
        gap = jnp.zeros((TILE - 2 * HALO, values.shape[1]), F32)
        out.append(parts[t][:TILE] + jnp.concatenate([before, gap, after], axis=0))
    return jnp.concatenate(out, axis=0)


def mortar_t_times(tiles_t, values):
    count = values.shape[0] // TILE
    none = jnp.zeros((HALO, values.shape[1]), BF16)
    fill = jnp.zeros((TILE - 2 * HALO, values.shape[1]), BF16)
    out = []
    for t in range(count):
        low, high = TILE * t, TILE * (t + 1)
        before = values[low - HALO : low] if t else none
        after = values[high : high + HALO] if t + 1 < count else none
        window = jnp.concatenate([values[low:high], before, after, fill], axis=0)
        out.append(dot(tiles_t[TILE * t : TILE * (t + 1), :], window))
    return jnp.concatenate(out, axis=0)


def unpacked(pack, t):
    edge = pack[160 * t : 160 * t + HALO, :].astype(F32)
    lane = lax.broadcasted_iota(jnp.int32, edge.shape, 1)
    above = jnp.where(lane < TILE // 2, edge, 0.0)
    below = jnp.where(lane < TILE // 2, 0.0, edge)
    middle = pack[160 * t + HALO : 160 * (t + 1), :].astype(F32)
    return jnp.concatenate([middle, above, below], axis=0)


def with_fill(tile):
    return jnp.concatenate([tile, jnp.zeros((TILE - 2 * HALO, TILE), F32)], axis=0)


class Moves:
    def __init__(self, sems):
        self.sems, self.used = sems, 0

    def start(self, source, target):
        copy = pltpu.make_async_copy(source, target, self.sems.at[self.used])
        self.used += 1
        copy.start()
        return copy


CHUNK = 256
SIDE = 32


def start_faces(moves, kinv, held, ms, first=0, end=None):
    copies = []
    for r in range(first, 2 * ms // CHUNK if end is None else end):
        row = r * CHUNK + (ms if r * CHUNK >= ms else 0)
        pair = []
        for to, at in ((0, 0), (ms, 2 * ms)):
            pair.append(
                moves.start(
                    kinv.at[pl.ds(row, CHUNK), pl.ds(at, ms)],
                    held.at[pl.ds(r * CHUNK, CHUNK), pl.ds(to, ms)],
                )
            )
        copies.append(pair)
    return copies


def solved(copies, held, load, fixed, zt, um, us, ms, start=0):
    for r, pair in enumerate(copies, start):
        for copy in pair:
            copy.wait()
        row = r * CHUNK
        u = (dot(held[row : row + CHUNK, :], load) + fixed[row : row + CHUNK, :]).astype(BF16)
        if row < ms:
            um[row : row + CHUNK, :] = u
        else:
            us[row - ms : row - ms + CHUNK, :] = u
    if zt is None:
        return None
    both = dot(zt[:, :ms], um[...]) + dot(zt[:, ms:], us[...])
    return both[:24] + both[24:]


def loads_of(push, scaled, loads_m, loads_s):
    master = (-push.astype(F32) - loads_m.astype(F32)).astype(BF16)
    slave = (scaled - loads_s.astype(F32)).astype(BF16)
    return jnp.concatenate([master, slave], axis=0)


def pack_kernel(mortar, seg, field, modes, coarse, weights, cand, out, behind):
    ms = mortar.shape[0]
    nr = coarse.shape[0]
    rigid = rows_of(modes, nr)
    count = ms // TILE
    ids = seg[...].astype(F32)
    ids_col = column(ids)
    none = jnp.zeros((HALO, TILE), F32)

    def masked(low, high, t):
        own = slice(TILE * t, TILE * (t + 1))
        same = ids_col[low:high] == ids[:, own]
        return jnp.where(same, mortar[low:high, own].astype(F32), 0.0)

    tiles = []
    for t in range(count):
        low, high = TILE * t, TILE * (t + 1)
        middle = masked(low, high, t)
        above = masked(low - HALO, low, t) if t else none
        below = masked(high, high + HALO, t) if t + 1 < count else none
        out[160 * t : 160 * t + HALO, :] = (above + below).astype(BF16)
        out[160 * t + HALO : 160 * (t + 1), :] = middle.astype(BF16)
        tile = jnp.concatenate([middle, above, below], axis=0)
        tiles.append(with_fill(tile).T.astype(BF16))
    push = mortar_t_times(jnp.concatenate(tiles, axis=0), field[...].astype(BF16))
    out[160 * count : 160 * count + ms, :] = push.astype(BF16)

    behind[...] = jnp.zeros_like(behind)
    behind[0:nr, :] = rigid[:, :ms]
    behind[8 : 8 + nr, :] = coarse[...]
    for t in range(count):
        own = slice(TILE * t, TILE * (t + 1))
        chosen = jnp.zeros((1, TILE), F32)
        if TILE * (t + 1) <= cand.shape[1]:
            chosen = cand[:, own].astype(F32)
        lanes = slice(ms + TILE * t, ms + TILE * (t + 1))
        pad = jnp.zeros((8 - nr, TILE), F32)
        rows = [rigid[:, lanes], pad, coarse[:, own], pad, weights[:, own], chosen]
        value = jnp.concatenate(rows + [jnp.zeros((SIDE - 18, TILE), F32)], axis=0)
        high, low = halves(value)
        base = 160 * count + ms + 2 * SIDE * t
        out[base : base + SIDE, :] = high.astype(BF16)
        out[base + SIDE : base + 2 * SIDE, :] = low.astype(BF16)


def side_rows(pack_p, ms):
    count = ms // TILE
    out = []
    for t in range(count):
        base = 160 * count + ms + 2 * SIDE * t
        high = pack_p[base : base + SIDE, :].astype(F32)
        out.append(high + pack_p[base + SIDE : base + 2 * SIDE, :].astype(F32))
    return jnp.concatenate(out, axis=1)


def fixed_kernel(loads, kinv, out, held, sems):
    ms = loads.shape[0] // 3
    moves = Moves(sems)
    copies = []
    for r in range(2 * ms // CHUNK):
        row = r * CHUNK + (ms if r * CHUNK >= ms else 0)
        copies.append(
            moves.start(
                kinv.at[pl.ds(row, CHUNK), pl.ds(ms, ms)], held.at[pl.ds(r * CHUNK, CHUNK), :]
            )
        )
    for r, copy in enumerate(copies):
        copy.wait()
        out[r * CHUNK : (r + 1) * CHUNK, :] = -dot(
            held[r * CHUNK : (r + 1) * CHUNK, :], loads[ms : 2 * ms, :]
        )


def setup_kernel(*refs):
    names, results = 8, 11
    kinv = refs[names]
    far_outs = refs[names + 1 : names + 1 + results]
    rest = refs[names + 1 + results :]
    local, rest = rest[:names], rest[names:]
    outs, rest = rest[:results], rest[results:]
    held, rows, modes, modes_p, um, us, long, sems = rest
    pack_p, weights, rigid_row, side_n, pack, field, loads, fixed = local
    tiles_s, tiles_p, tiles_pt, side_p, zt, md, md_p, near, far, resid, klt = outs
    ms = weights.shape[1]
    nr = rigid_row.shape[1] // (2 * ms)
    odd = is_odd()
    count = ms // TILE
    span = TILE + 2 * HALO
    moves = Moves(sems)
    arrive = [moves.start(a, b) for a, b in zip(refs[:names], local)]
    copies = start_faces(moves, kinv, held, ms)
    leaving = []

    def wait(*which):
        for n in which:
            arrive[n].wait()

    def leave(*which):
        for n in which:
            leaving.append(moves.start(outs[n], far_outs[n]))

    wait(0)
    for t in range(count):
        tile = unpacked(pack_p, t)
        tiles_p[span * t : span * (t + 1), :] = tile.astype(BF16)
        tiles_pt[TILE * t : TILE * (t + 1), :] = with_fill(tile).T.astype(BF16)
    side_p[...] = side_rows(pack_p, ms)
    leave(1, 2, 3)

    wait(1, 2, 3, 4)
    rigid = rows_of(rigid_row, nr)
    for t in range(count):
        tiles_s[span * t : span * (t + 1), :] = unpacked(pack, t).astype(BF16)
    leave(0)

    def through(tiles, values):
        rows[...] = jnp.zeros_like(rows)
        high, low = halves(values)
        rows[0:nr, :] = high
        rows[8 : 8 + nr, :] = low
        moved = mortar_times(tiles, rows[...].T.astype(BF16)).T
        return moved[0:nr] + moved[8 : 8 + nr]

    modes[...] = jnp.zeros_like(modes)
    modes_p[...] = jnp.zeros_like(modes_p)
    modes[nr : 2 * nr, :] = rigid[:, ms:] * weights[...]
    modes[2 * nr : 3 * nr, :] = -through(tiles_s, side_n[0:nr, :])
    modes_p[0:nr, :] = side_p[0:nr, :] * side_p[16:17, :]
    modes_p[nr : 2 * nr, :] = -through(tiles_p, rigid[:, :ms])

    def placed(values):
        later = jnp.concatenate([values[18:24], values[0:18]], axis=0)
        return jnp.where(odd, later, values)

    def stacked(values):
        high, low = halves(values)
        rows[...] = jnp.zeros_like(rows)
        rows[0:24, :] = high
        rows[32:56, :] = low
        rows[64:88, :] = high
        return rows[...].T.astype(BF16)

    own = placed(modes[...])
    md[...] = stacked(own)
    columns = stacked(placed(modes_p[...]))
    md_p[...] = columns
    leave(5, 6)
    pushed = mortar_t_times(tiles_pt, columns).T
    high, low = halves(-(pushed[0:24] + pushed[32:56]))
    zt[0:24, :ms] = high.astype(BF16)
    zt[24:48, :ms] = low.astype(BF16)
    high, low = halves(own * weights[...])
    zt[0:24, ms:] = high.astype(BF16)
    zt[24:48, ms:] = low.astype(BF16)
    leave(4)
    push = pack_p[160 * count : 160 * count + ms, :]
    wait(5, 6, 7)
    scaled = column(weights[...]) * field[...]
    load = loads_of(push, scaled, loads[:ms, :], loads[2 * ms :, :])
    long[...] = jnp.zeros_like(long)
    long[0:24, :] = zt[0:24, :].astype(F32)
    long[32:56, :] = zt[24:48, :].astype(F32)
    values = jnp.concatenate([load, long[...].T.astype(BF16)], axis=1)
    for r, pair in enumerate(copies):
        for copy in pair:
            copy.wait()
        row = r * CHUNK
        part = dot(held[row : row + CHUNK, :], values)
        u = (part[:, :TILE] + fixed[row : row + CHUNK, :]).astype(BF16)
        if row < ms:
            um[row : row + CHUNK, :] = u
        else:
            us[row - ms : row - ms + CHUNK, :] = u
        long[:, row : row + CHUNK] = part[:, TILE:].T
    both = dot(zt[:, :ms], um[...]) + dot(zt[:, ms:], us[...])
    resid[...] = both[:24] + both[24:]
    near[...] = jnp.where(odd, um[...], us[...])
    far[...] = jnp.where(odd, us[...], um[...])
    leave(9, 8, 7)
    high, low = halves(long[0:24, :] + long[32:56, :])
    klt[0:24, :] = high.astype(BF16)
    klt[24:48, :] = low.astype(BF16)
    leave(10)
    for copy in leaving:
        copy.wait()


def coarse_rows(coarse, side_p, side_n, source, cand, out, floors, rows):
    nr, width = coarse.shape
    rows[...] = jnp.zeros_like(rows)
    rows[0:nr, :] = side_p[8 : 8 + nr, :]
    rows[nr : 2 * nr, :] = coarse[...]
    rows[2 * nr : 3 * nr, :] = side_n[8 : 8 + nr, :]
    later = jnp.concatenate([rows[18:24, :], rows[0:18, :]], axis=0)
    high, low = halves(jnp.where(is_odd(), later, rows[...]))
    both = jnp.concatenate([high, low], axis=0).astype(BF16)
    count = width // TILE
    for n in range(out.shape[1] // CHUNK):
        near_by = [(n + k) % count for k in (-1, 0, 1)]
        left = jnp.concatenate([both[:, TILE * t : TILE * (t + 1)] for t in near_by], axis=1)
        wanted = source[:, n * CHUNK : (n + 1) * CHUNK]
        picks = []
        for t in near_by:
            index = lax.broadcasted_iota(jnp.int32, (TILE, CHUNK), 0) + TILE * t
            picks.append(jnp.where(index == wanted, 1.0, 0.0).astype(BF16))
        out[:, n * CHUNK : (n + 1) * CHUNK] = dot(left, jnp.concatenate(picks, axis=0)).astype(
            BF16
        )

    floors[...] = jnp.zeros_like(floors)
    chosen = (cand[...].astype(F32), side_p[17:18, : cand.shape[1]])
    for t in range(floors.shape[1] // TILE):
        place = lax.broadcasted_iota(jnp.int32, (TILE, cand.shape[1]), 0) + TILE * t
        for n, which in enumerate(chosen):
            hit = jnp.where(place.astype(F32) == which, 1.0, 0.0)
            found = jnp.broadcast_to(jnp.max(hit, axis=1, keepdims=True), (TILE, TILE)).T
            floors[n : n + 1, TILE * t : TILE * (t + 1)] = jnp.where(
                found[0:1] > 0.0, 0.0, -jnp.inf
            )


def pair_kernel(resid, other, out):
    pair = (resid[...] + other[...]).astype(BF16)
    out[...] = jnp.broadcast_to(pair[None], out.shape)


def last_kernel(slave, um_n, tiles_s, grad):
    grad[...] = slave[...] - mortar_times(tiles_s, um_n[...])


def dot_rows(left, right):
    return lax.dot_general(left, right, (((1,), (1,)), ((), ())), preferred_element_type=F32)


def forms_kernel(
    zt, md, klt, coarse, side_p, side_n, source, cand, near,
    mrows, forms, coarse_of, floors,
    square, rows,
):
    del near
    ms = md.shape[0]
    coarse_rows(coarse, side_p, side_n, source, cand, coarse_of, floors, rows)
    mrows[...] = md[...].astype(F32).T[0:64].astype(BF16)

    def form(at, product):
        square[...] = jnp.zeros_like(square)
        square[0:24, 0:64] = product[0:24] + product[32:56]
        turned = square[...].T
        high, low = halves(turned[0:24] + turned[32:56])
        square[...] = jnp.zeros_like(square)
        square[0:24, :] = high
        square[32:56, :] = low
        square[64:88, :] = high
        forms[at : at + 24, :] = square[...].T[0:24].astype(BF16)

    gap = jnp.zeros((8, 2 * ms), BF16)
    left = jnp.concatenate([zt[0:24, :], gap, zt[24:48, :], gap], axis=0)
    right = jnp.concatenate([klt[0:24, :], gap, klt[24:48, :], gap], axis=0)
    form(0, dot_rows(mrows[...], mrows[...]))
    form(24, dot_rows(left, right))


def gradient_kernel(*refs):
    names = 12
    kinv, _, g_out, gp_out, stats = refs[names : names + 5]
    held = refs[names + 5]
    local = refs[names + 6 : 2 * names + 6]
    g, gp, solution, sems = refs[2 * names + 6 :]
    ms = g.shape[0]
    moves = Moves(sems)
    arrive = [moves.start(a, b) for a, b in zip(refs[:9], local[:9])]
    copies = start_faces(moves, kinv, held, ms)
    arrive += [moves.start(a, b) for a, b in zip(refs[9:names], local[9:])]
    weights, side_p, near, far, near_r, far_r, tiles_p, tiles_pt, tiles_s, mrows, zt, klt = local

    def wait(*which):
        for n in which:
            arrive[n].wait()

    wait(0, 1, 2, 3, 4, 5, 6)
    odd = is_odd()
    um, us = jnp.where(odd, near[...], far[...]), jnp.where(odd, far[...], near[...])
    um_n = jnp.where(odd, far_r[...], near_r[...])
    us_p = jnp.where(odd, near_r[...], far_r[...])
    wcol = column(weights[...])
    gp[...] = column(side_p[16:17, :]) * us_p.astype(F32) - mortar_times(tiles_p, um)
    out_p = moves.start(gp, gp_out)
    wait(7)
    master = (-mortar_t_times(tiles_pt, gp[...].astype(BF16))).astype(BF16)
    wait(8)
    g[...] = wcol * us.astype(F32) - mortar_times(tiles_s, um_n)
    out_s = moves.start(g, g_out)
    load = jnp.concatenate([master, (wcol * g[...]).astype(BF16)], axis=0)
    curve = jnp.zeros((CHUNK, TILE), F32)
    for r, pair in enumerate(copies):
        for copy in pair:
            copy.wait()
        row = r * CHUNK
        part = dot(held[row : row + CHUNK, :], load)
        solution[row : row + CHUNK, :] = part
        curve += load[row : row + CHUNK].astype(F32) * part
    wait(9, 10, 11)
    stats[...] = jnp.zeros_like(stats)
    stats[0:1, :] = jnp.sum(g[...] * g[...], axis=0, keepdims=True)
    stats[1:2, :] = jnp.sum(curve, axis=0, keepdims=True)
    high, low = halves(g[...])
    first = dot(mrows[...], high.astype(BF16))
    second = dot(mrows[0:32, :], low.astype(BF16))
    stats[8:32, :] = first[0:24] + first[32:56] + second[0:24]
    high, low = halves(solution[...])
    first = dot(zt[...], high.astype(BF16)) + dot(klt[...], load)
    second = dot(zt[0:32, :], low.astype(BF16))
    stats[32:56, :] = first[0:24] + first[24:48] + second[0:24]
    out_p.wait()
    out_s.wait()


def project_kernel(every, coarse, forms, stats, stack, sums):
    both = dot(coarse[...], every[...].reshape(coarse.shape[1], TILE))
    c = both[:24] + both[24:]
    high, low = halves(c)
    gap = jnp.zeros((8, TILE), F32)
    rest = jnp.zeros((TILE - 88, TILE), F32)
    operand = jnp.concatenate([high, gap, high, gap, low, rest], axis=0).astype(BF16)
    stack[...] = operand
    moved = dot(forms[...], operand)
    norm = stats[0:1, :] + jnp.sum(
        c * (moved[0:24] - 2.0 * stats[8:32, :]), axis=0, keepdims=True
    )
    curve = stats[1:2, :] + jnp.sum(c * (moved[24:48] - stats[32:56, :]), axis=0, keepdims=True)
    total = jnp.concatenate([norm, curve], axis=0)
    sums[...] = jnp.broadcast_to(total[None], sums.shape)


def direction_kernel(stack, g, gp, md, md_p, d, dp):
    d[...] = g[...] - dot(md[...], stack[...])
    dp[...] = gp[...] - dot(md_p[...], stack[...])


def marker_kernel(near, out):
    del near
    out[...] = jnp.zeros_like(out)


def step_kernel(final, *refs):
    names = 10
    loads, kinv = refs[names : names + 2]
    y_out, yp_out, near_out, far_out, resid_out = refs[names + 2 : names + 7]
    held = refs[names + 7]
    local = refs[names + 8 : 2 * names + 8]
    loads_m, loads_s, um, us, near, far, resid, sems = refs[2 * names + 8 :]
    weights, floors, sums, field_p, dp, tiles_pt, field, d, zt, fixed = local[:10]
    ms = d.shape[0]
    moves = Moves(sems)
    arrive = [moves.start(refs[n], local[n]) for n in range(8)]
    arrive_m = moves.start(loads.at[pl.ds(0, ms), :], loads_m)
    arrive_s = moves.start(loads.at[pl.ds(2 * ms, ms), :], loads_s)
    arrive += [moves.start(refs[n], local[n]) for n in range(8, 10)]
    copies = start_faces(moves, kinv, held, ms, 0, ms // CHUNK if final else None)

    def wait(*which):
        for n in which:
            arrive[n].wait()

    wait(0, 1)
    wcol = column(weights[...])
    floor, floor_p = column(floors[0:1, :]), column(floors[1:2, :])
    wait(2)
    total = jnp.sum(sums[...], axis=0)
    step = total[0:1] / total[1:2]
    wait(3, 4)
    field_p[...] = jnp.maximum(field_p[...] - step * dp[...], floor_p)
    out_p = None if final else moves.start(field_p, yp_out)
    wait(5)
    push = mortar_t_times(tiles_pt, field_p[...].astype(BF16)).astype(BF16)
    wait(6, 7)
    field[...] = jnp.maximum(field[...] - step * d[...], floor)
    out_s = moves.start(field, y_out)
    arrive_m.wait()
    arrive_s.wait()
    load = loads_of(push, wcol * field[...], loads_m[...], loads_s[...])
    wait(8, 9)
    if final:
        near[...] = load[:ms]
        far[...] = load[ms:]
        outs = [moves.start(near, near_out), moves.start(far, far_out)]
        solved(copies, held, load, fixed, None, um, us, ms)
        outs += [out_s, moves.start(um, yp_out)]
    else:
        resid[...] = solved(copies, held, load, fixed, zt, um, us, ms)
        odd = is_odd()
        near[...] = jnp.where(odd, um[...], us[...])
        far[...] = jnp.where(odd, us[...], um[...])
        outs = [moves.start(far, far_out), moves.start(near, near_out)]
        outs += [out_p, out_s, moves.start(resid, resid_out)]
    for copy in outs:
        copy.wait()


def slave_kernel(load_m, load_s, weights, fixed, kinv, out, held, us, sems):
    ms = weights.shape[1]
    copies = start_faces(Moves(sems), kinv, held, ms, ms // CHUNK)
    load = jnp.concatenate([load_m[...], load_s[...]], axis=0)
    solved(copies, held, load, fixed, None, None, us, ms, ms // CHUNK)
    out[...] = column(weights[...]) * us[...].astype(F32)


def shape(dims, dtype):
    return jax.ShapeDtypeStruct(dims, dtype)


def kernel_call(body, outs, *operands, anywhere=(), anywhere_out=(), scratch=(), flops=0):
    here = pl.BlockSpec(memory_space=pltpu.VMEM)
    far = pl.BlockSpec(memory_space=pl.ANY)
    moved = sum(int(np.prod(o.shape)) * o.dtype.itemsize for o in list(operands) + list(outs))
    return pl.pallas_call(
        body,
        out_shape=tuple(outs),
        in_specs=[far if n in anywhere else here for n in range(len(operands))],
        out_specs=tuple(far if n in anywhere_out else here for n in range(len(outs))),
        scratch_shapes=list(scratch),
        compiler_params=pltpu.CompilerParams(vmem_limit_bytes=64 * MIB),
        cost_estimate=pl.CostEstimate(flops=flops, bytes_accessed=moved, transcendentals=0),
    )(*operands)


def on_device(
    inverse_blocks,
    primal_loads,
    mortar_values,
    segment_ids,
    slave_weights,
    rigid_modes,
    coarse_inverse,
    candidates,
    start_multipliers,
):
    ms = mortar_values.shape[1]
    nr = rigid_modes.shape[1]
    nc = coarse_inverse.shape[1]
    lc = start_multipliers.shape[2]
    sub, grp = lax.axis_size("sub"), lax.axis_size("grp")
    chips = sub * grp // 2
    kinv = inverse_blocks[0]
    loads = primal_loads[0]
    rigid = rigid_modes.reshape(1, -1)
    field = start_multipliers[0]
    count = ms // TILE
    face = lambda dtype: shape((ms, lc), dtype)
    kff = pltpu.VMEM((2 * ms, 2 * ms), BF16)
    chunks = 2 * ms // CHUNK

    pack, behind = kernel_call(
        pack_kernel,
        [shape(((160 + 2 * SIDE) * count + ms, lc), BF16), shape((16, ms), F32)],
        mortar_values[0],
        segment_ids,
        field,
        rigid,
        coarse_inverse,
        slave_weights,
        candidates,
    )
    pack_p = shifted(pack, 1)
    side_n = shifted(behind, -1)
    field_p = shifted(field, 1)
    (fixed,) = kernel_call(
        fixed_kernel,
        [shape((2 * ms, lc), F32)],
        loads,
        kinv,
        anywhere=(1,),
        scratch=[pltpu.VMEM((2 * ms, ms), BF16), pltpu.SemaphoreType.DMA((chunks,))],
        flops=4 * ms * ms * lc,
    )
    outs = [
        shape((TILE_ROWS * count, TILE), BF16),
        shape((TILE_ROWS * count, TILE), BF16),
        shape((ms, 2 * TILE), BF16),
        shape((SIDE, ms), F32),
        shape((48, 2 * ms), BF16),
        face(BF16),
        face(BF16),
        face(BF16),
        face(BF16),
        shape((24, lc), F32),
        shape((48, 2 * ms), BF16),
    ]
    operands = (pack_p, slave_weights, rigid, side_n, pack, field, loads, fixed)
    (tiles_s, tiles_p, tiles_pt, side_p, zt, md, md_p, near, far, resid, klt) = kernel_call(
        setup_kernel,
        outs,
        *operands,
        kinv,
        anywhere=range(len(operands) + 1),
        anywhere_out=range(len(outs)),
        scratch=[pltpu.VMEM(o.shape, o.dtype) for o in operands]
        + [pltpu.VMEM(o.shape, o.dtype) for o in outs]
        + [
            kff,
            pltpu.VMEM((TILE, ms), F32),
            pltpu.VMEM((24, ms), F32),
            pltpu.VMEM((24, ms), F32),
            pltpu.VMEM((ms, lc), BF16),
            pltpu.VMEM((ms, lc), BF16),
            pltpu.VMEM((TILE, 2 * ms), F32),
            pltpu.SemaphoreType.DMA((len(operands) + len(outs) + 2 * chunks,)),
        ],
        flops=8 * ms * ms * lc,
    )

    chip, group, spot, mode = np.meshgrid(
        np.arange(sub // 2), np.arange(grp), np.arange(4), np.arange(nr), indexing="ij"
    )
    source = (((2 * chip + spot - 1) % sub) * grp + group) * nr + mode
    source = jnp.asarray(source.reshape(1, -1), jnp.int32)
    mrows, forms, coarse, floors = kernel_call(
        forms_kernel,
        [
            shape((64, ms), BF16),
            shape((48, TILE), BF16),
            shape((48, source.shape[1]), BF16),
            shape((8, ms), F32),
        ],
        zt,
        md,
        klt,
        coarse_inverse,
        side_p,
        side_n,
        source,
        candidates,
        near,
        anywhere=(8,),
        scratch=[pltpu.VMEM((TILE, TILE), F32), pltpu.VMEM((24, nc), F32)],
        flops=10**11,
    )

    same_core = [
        [(2 * m + core) * grp + z for m in range(sub // 2) for z in range(grp)]
        for core in range(2)
    ]
    for turn in range(STEPS):
        (pieces,) = kernel_call(
            pair_kernel, [shape((chips, 24, lc), BF16)], resid, swapped(resid)
        )
        every = lax.all_to_all(
            pieces, AXES, 0, 0, tiled=True, axis_index_groups=same_core
        )
        far_r = swapped_out(far)
        near_r = swapped(near)
        (marker,) = kernel_call(
            marker_kernel, [shape((8, TILE), F32)], near, anywhere=(0,), flops=10**12
        )
        operands = (
            slave_weights, side_p, near, far, near_r, far_r, tiles_p, tiles_pt, tiles_s,
            mrows, zt, klt,
        )
        g, g_p, stats = kernel_call(
            gradient_kernel,
            [face(F32), face(F32), shape((64, lc), F32)],
            *operands,
            kinv,
            marker,
            anywhere=range(len(operands) + 2),
            anywhere_out=(0, 1),
            scratch=[kff]
            + [pltpu.VMEM(o.shape, o.dtype) for o in operands]
            + [
                pltpu.VMEM((ms, lc), F32),
                pltpu.VMEM((ms, lc), F32),
                pltpu.VMEM((2 * ms, lc), F32),
                pltpu.SemaphoreType.DMA((len(operands) + 2 * chunks + 2,)),
            ],
            flops=8 * ms * ms * lc,
        )
        stack, sums = kernel_call(
            project_kernel,
            [shape((TILE, lc), BF16), shape((2 * chips, 2, lc), F32)],
            every, coarse, forms, stats,
            flops=2 * 48 * every.shape[0] * every.shape[1] * lc,
        )
        d, d_p = kernel_call(
            direction_kernel,
            [face(F32), face(F32)],
            stack, g, g_p, md, md_p,
            flops=4 * ms * TILE * lc,
        )
        totals = lax.all_to_all(sums, AXES, 0, 0, tiled=True)
        operands = (
            slave_weights, floors, totals, field_p, d_p, tiles_pt, field, d, zt, fixed,
        )
        final = turn == STEPS - 1
        field, field_p, near, far, resid = kernel_call(
            functools.partial(step_kernel, final),
            [
                face(F32),
                face(BF16 if final else F32),
                face(BF16),
                face(BF16),
                shape((24, lc), F32),
            ],
            *operands,
            loads,
            kinv,
            anywhere=range(len(operands) + 2),
            anywhere_out=(0, 1, 2, 3, 4),
            scratch=[kff]
            + [pltpu.VMEM(o.shape, o.dtype) for o in operands]
            + [pltpu.VMEM((ms, lc), BF16)] * 6
            + [
                pltpu.VMEM((24, lc), F32),
                pltpu.SemaphoreType.DMA((len(operands) + 2 * chunks + 7,)),
            ],
            flops=8 * ms * ms * lc,
        )
    um_n = shifted(field_p, -1)
    (slave,) = kernel_call(
        slave_kernel,
        [face(F32)],
        near, far, slave_weights, fixed, kinv,
        anywhere=(4,),
        scratch=[kff, pltpu.VMEM((ms, lc), BF16), pltpu.SemaphoreType.DMA((chunks,))],
        flops=10**11,
    )
    (gradient,) = kernel_call(
        last_kernel, [face(F32)], slave, um_n, tiles_s, flops=2 * 192 * ms * lc
    )
    return (field[None], gradient[None])


def solution(mesh):
    placed = (
        P(AXES, None, None),
        P(AXES, None, None),
        P(AXES, None, None),
        P(AXES, None),
        P(AXES, None),
        P(AXES, None, None),
        P(AXES, None),
        P(AXES, None),
        P(AXES, None, None),
    )
    return jax.shard_map(
        on_device,
        mesh=mesh,
        in_specs=placed,
        out_specs=(P(AXES, None, None), P(AXES, None, None)),
        check_vma=False,
    )
```

profile of v0, /device:TPU:1, one launch (start us, length us, event | category | flops | bytes accessed | tf_op | source)
XLA Modules:
  0.0 170.0 jit_solution(6444940791867191545)
XLA Ops:
  0.6 2.7 %shard_map.113 = (bf16[2112,128]{1,0:T(8,128)(2,1)}, f32[16,768]{1,0:T(8,128)}) custom-call(bf16[768,768]{1,0:T(8,128)(2,1)} %bitcast.25, s32[1,768]{1,0:T(1,128)} %seg.1, f32[768,128]{1,0:T(8,128)} %bitcast.21, f32[1,9216]{1,0:T(1,128)} %bitcast.27, f32[6,768]{1,0:T(8,128)} %coarse.3, f32[1,768]{1,0:T(1,128)} %weights.3, s32[1,384]{1,0:T(1,128)} %cand.3), custom_call_target="tpu_custom_call" | custom-call | bytes 2225664 | tf_op jit(solution)/shard_map/pallas_call | solution.py:570
  3.4 2.6 %collective-permute-start = (bf16[2112,128]{1,0:T(8,128)(2,1)}, bf16[2112,128]{1,0:T(8,128)(2,1)}, u32[]{:S(2)}, u32[]{:S(2)}) collective-permute-start(bf16[2112,128]{1,0:T(8,128)(2,1)} %get-tuple-element.54.refs_4_), channel_id=1, source_target_pairs={{124,0},{0,4},{4,8},{8,12},{12,16},{16,20},{20,24},{24,28},{28,32}... | collective-permute-start | bytes 1622024 | tf_op jit(solution)/shard_map/ppermute | solution.py:22
  7.7 4.7 %shard_map.114.refs_7_.refs_9_.fixed = f32[1536,128]{1,0:T(8,128)} custom-call(bf16[2304,128]{1,0:T(8,128)(2,1)} %bitcast.16, bf16[2304,2304]{1,0:T(8,128)(2,1)} %bitcast.7), custom_call_target="tpu_custom_call" | custom-call | flops 301989888 | bytes 11993088 | tf_op jit(solution)/shard_map/pallas_call | solution.py:570
  12.6 7.5 %shard_map.115 = (bf16[1152,128]{1,0:T(8,128)(2,1)}, bf16[1152,128]{1,0:T(8,128)(2,1)}, bf16[768,256]{1,0:T(8,128)(2,1)}, f32[32,768]{1,0:T(8,128)}, bf16[48,153...) custom-call(bf16[2112,128]{1,0:T(8,128)(2,1)} %collective-permute-do, ...), custom_call_target="tpu_custom_call" | custom-call | flops 603979776 | bytes 15731712 | tf_op jit(solution)/shard_map/pallas_call | solution.py:570
  20.1 4.7 %collective-permute-start.2 = (f32[24,128]{1,0:T(8,128)}, f32[24,128]{1,0:T(8,128)}, u32[]{:S(2)}, u32[]{:S(2)}) collective-permute-start(f32[24,128]{1,0:T(8,128)} %get-tuple-element.62.resid), channel_id=1, source_target_pairs={{4,0},{0,4},{12,8},{8,12},{20,16},{16,20},{28,24},{24,28},{36,32},... | collective-permute-start | bytes 36872 | tf_op jit(solution)/shard_map/ppermute | solution.py:27
  27.5 10.7 %all-to-all-start = ((bf16[64,24,128]{2,1,0:T(8,128)(2,1)}), bf16[64,24,128]{2,1,0:T(8,128)(2,1)}, u32[]{:S(2)}, u32[]{:S(2)}) async-start(bf16[64,24,128]{2,1,0:T(8,128)(2,1)} %shard_map.117), calls=%async_computation | async-start | bytes 786432 | tf_op jit(solution)/shard_map/all_to_all | solution.py:701
  38.2 2.7 %shard_map.116 = (bf16[64,768]{1,0:T(8,128)(2,1)}, bf16[48,128]{1,0:T(8,128)(2,1)}, bf16[48,1536]{1,0:T(8,128)(2,1)}, f32[8,768]{1,0:T(8,128)}) custom-call(bf16[48,1536]{1,0:T(8,128)(2,1)} %get-tuple-element.56.zt.refs_10_.refs_8_, bf16[768,128]{1,0:T(8,128)(2,1)} %get-tuple-element.57.md, bf16[48,1536]{1,0:T(8,128)(2,1)} %get-tuple-element.58.klt.refs_11_, ...), custom_call_target="tpu_custom_call" | custom-call | flops 99999997952 | bytes 1144320 | tf_op jit(solution)/shard_map/pallas_call | solution.py:570
  40.9 5.8 %shard_map.119 = (f32[768,128]{1,0:T(8,128)}, f32[768,128]{1,0:T(8,128)}, f32[64,128]{1,0:T(8,128)}) custom-call(f32[1,768]{1,0:T(1,128)} %weights.3, f32[32,768]{1,0:T(8,128)} %get-tuple-element.59.side_p.refs_1_, bf16[768,128]{1,0:T(8,128)(2,1)} %get-tuple-element.60.near.refs_2_, bf16[768,128]{1,0:T(8,128)(2,1)} %get-tuple-element.65.refs_3_, ...), custom_call_target="tpu_custom_call" | custom-call | flops 603979776 | bytes 13704192 | tf_op jit(solution)/shard_map/pallas_call | solution.py:570
  46.7 2.6 %all-to-all-done.every = bf16[64,24,128]{2,1,0:T(8,128)(2,1)} async-done(((bf16[64,24,128]{2,1,0:T(8,128)(2,1)}), bf16[64,24,128]{2,1,0:T(8,128)(2,1)}, u32[]{:S(2)}, u32[]{:S(2)}) %all-to-all-start) | async-done | bytes 393248 | tf_op jit(solution)/shard_map/all_to_all | solution.py:701
  49.3 2.1 %shard_map.120 = (bf16[128,128]{1,0:T(8,128)(2,1)}, f32[128,2,128]{2,1,0:T(2,128)}) custom-call(bf16[64,24,128]{2,1,0:T(8,128)(2,1)} %all-to-all-done.every, bf16[48,1536]{1,0:T(8,128)(2,1)} %get-tuple-element.63.coarse, bf16[48,128]{1,0:T(8,128)(2,1)} %get-tuple-element.64.forms, f32[64,128]{1,0:T(8,128)} %get-tuple-element.70.stats), custom_call_target="tpu_custom_call" | custom-call | flops 18874368 | bytes 749568 | tf_op jit(solution)/shard_map/pallas_call | solution.py:570
  51.4 6.6 %all-to-all-start.1 = ((f32[128,2,128]{2,1,0:T(2,128)}), f32[128,2,128]{2,1,0:T(2,128)}, u32[]{:S(2)}, u32[]{:S(2)}) async-start(f32[128,2,128]{2,1,0:T(2,128)} %get-tuple-element.71), calls=%async_computation.1 | async-start | bytes 262144 | tf_op jit(solution)/shard_map/all_to_all | solution.py:743
  57.9 2.4 %shard_map.121 = (f32[768,128]{1,0:T(8,128)}, f32[768,128]{1,0:T(8,128)}) custom-call(bf16[128,128]{1,0:T(8,128)(2,1)} %get-tuple-element.72.stack, f32[768,128]{1,0:T(8,128)} %get-tuple-element.73.g, f32[768,128]{1,0:T(8,128)} %get-tuple-element.74.gp, bf16[768,128]{1,0:T(8,128)(2,1)} %get-tuple-element.57.md, bf16[768,128]{1,0:T(8,128)(2,1)} %get-tuple-element.75.md_p), custom_call_target="tpu_custom_call" | custom-call | flops 50331648 | bytes 1998848 | tf_op jit(solution)/shard_map/pallas_call | solution.py:570
  60.4 7.4 %all-to-all-done.1.refs_2_ = f32[128,2,128]{2,1,0:T(2,128)} async-done(((f32[128,2,128]{2,1,0:T(2,128)}), f32[128,2,128]{2,1,0:T(2,128)}, u32[]{:S(2)}, u32[]{:S(2)}) %all-to-all-start.1) | async-done | bytes 131104 | tf_op jit(solution)/shard_map/all_to_all | solution.py:743
  67.8 5.6 %shard_map.122 = (f32[768,128]{1,0:T(8,128)}, f32[768,128]{1,0:T(8,128)}, bf16[768,128]{1,0:T(8,128)(2,1)}, bf16[768,128]{1,0:T(8,128)(2,1)}, f32[24,128]{1,0:T(8,128)}) custom-call(f32[1,768]{1,0:T(1,128)} %weights.3, f32[8,768]{1,0:T(8,128)} %get-tuple-element.61.refs_1_, f32[128,2,128]{2,1,0:T(2,128)} %all-to-all-done.1.refs_2_, ...), custom_call_target="tpu_custom_call" | custom-call | flops 603979776 | bytes 15457280 | tf_op jit(solution)/shard_map/pallas_call | solution.py:570
  77.4 6.2 %all-to-all-start.2 = ((bf16[64,24,128]{2,1,0:T(8,128)(2,1)}), bf16[64,24,128]{2,1,0:T(8,128)(2,1)}, u32[]{:S(2)}, u32[]{:S(2)}) async-start(bf16[64,24,128]{2,1,0:T(8,128)(2,1)} %shard_map.123), calls=%async_computation.2 | async-start | bytes 786432 | tf_op jit(solution)/shard_map/all_to_all | solution.py:701
  84.2 5.8 %shard_map.125 = (f32[768,128]{1,0:T(8,128)}, f32[768,128]{1,0:T(8,128)}, f32[64,128]{1,0:T(8,128)}) custom-call(f32[1,768]{1,0:T(1,128)} %weights.3, f32[32,768]{1,0:T(8,128)} %get-tuple-element.59.side_p.refs_1_, bf16[768,128]{1,0:T(8,128)(2,1)} %get-tuple-element.79.near.refs_2_, bf16[768,128]{1,0:T(8,128)(2,1)} %get-tuple-element.80.refs_3_, ...), custom_call_target="tpu_custom_call" | custom-call | flops 603979776 | bytes 13704192 | tf_op jit(solution)/shard_map/pallas_call | solution.py:570
  90.0 4.3 %all-to-all-done.2.every = bf16[64,24,128]{2,1,0:T(8,128)(2,1)} async-done(((bf16[64,24,128]{2,1,0:T(8,128)(2,1)}), bf16[64,24,128]{2,1,0:T(8,128)(2,1)}, u32[]{:S(2)}, u32[]{:S(2)}) %all-to-all-start.2) | async-done | bytes 393248 | tf_op jit(solution)/shard_map/all_to_all | solution.py:701
  94.3 2.1 %shard_map.126 = (bf16[128,128]{1,0:T(8,128)(2,1)}, f32[128,2,128]{2,1,0:T(2,128)}) custom-call(bf16[64,24,128]{2,1,0:T(8,128)(2,1)} %all-to-all-done.2.every, bf16[48,1536]{1,0:T(8,128)(2,1)} %get-tuple-element.63.coarse, bf16[48,128]{1,0:T(8,128)(2,1)} %get-tuple-element.64.forms, f32[64,128]{1,0:T(8,128)} %get-tuple-element.81.stats), custom_call_target="tpu_custom_call" | custom-call | flops 18874368 | bytes 749568 | tf_op jit(solution)/shard_map/pallas_call | solution.py:570
  96.3 6.5 %all-to-all-start.3 = ((f32[128,2,128]{2,1,0:T(2,128)}), f32[128,2,128]{2,1,0:T(2,128)}, u32[]{:S(2)}, u32[]{:S(2)}) async-start(f32[128,2,128]{2,1,0:T(2,128)} %get-tuple-element.82), calls=%async_computation.3 | async-start | bytes 262144 | tf_op jit(solution)/shard_map/all_to_all | solution.py:743
  102.8 2.4 %shard_map.127 = (f32[768,128]{1,0:T(8,128)}, f32[768,128]{1,0:T(8,128)}) custom-call(bf16[128,128]{1,0:T(8,128)(2,1)} %get-tuple-element.84.stack, f32[768,128]{1,0:T(8,128)} %get-tuple-element.85.g, f32[768,128]{1,0:T(8,128)} %get-tuple-element.86.gp, bf16[768,128]{1,0:T(8,128)(2,1)} %get-tuple-element.57.md, bf16[768,128]{1,0:T(8,128)(2,1)} %get-tuple-element.75.md_p), custom_call_target="tpu_custom_call" | custom-call | flops 50331648 | bytes 1998848 | tf_op jit(solution)/shard_map/pallas_call | solution.py:570
  105.2 7.6 %all-to-all-done.3.refs_2_ = f32[128,2,128]{2,1,0:T(2,128)} async-done(((f32[128,2,128]{2,1,0:T(2,128)}), f32[128,2,128]{2,1,0:T(2,128)}, u32[]{:S(2)}, u32[]{:S(2)}) %all-to-all-start.3) | async-done | bytes 131104 | tf_op jit(solution)/shard_map/all_to_all | solution.py:743
  112.8 5.6 %shard_map.128 = (f32[768,128]{1,0:T(8,128)}, f32[768,128]{1,0:T(8,128)}, bf16[768,128]{1,0:T(8,128)(2,1)}, bf16[768,128]{1,0:T(8,128)(2,1)}, f32[24,128]{1,0:T(8,128)}) custom-call(f32[1,768]{1,0:T(1,128)} %weights.3, f32[8,768]{1,0:T(8,128)} %get-tuple-element.61.refs_1_, f32[128,2,128]{2,1,0:T(2,128)} %all-to-all-done.3.refs_2_, ...), custom_call_target="tpu_custom_call" | custom-call | flops 603979776 | bytes 15457280 | tf_op jit(solution)/shard_map/pallas_call | solution.py:570
  122.4 6.4 %all-to-all-start.4 = ((bf16[64,24,128]{2,1,0:T(8,128)(2,1)}), bf16[64,24,128]{2,1,0:T(8,128)(2,1)}, u32[]{:S(2)}, u32[]{:S(2)}) async-start(bf16[64,24,128]{2,1,0:T(8,128)(2,1)} %shard_map.129), calls=%async_computation.4 | async-start | bytes 786432 | tf_op jit(solution)/shard_map/all_to_all | solution.py:701
  129.5 5.8 %shard_map.131 = (f32[768,128]{1,0:T(8,128)}, f32[768,128]{1,0:T(8,128)}, f32[64,128]{1,0:T(8,128)}) custom-call(f32[1,768]{1,0:T(1,128)} %weights.3, f32[32,768]{1,0:T(8,128)} %get-tuple-element.59.side_p.refs_1_, bf16[768,128]{1,0:T(8,128)(2,1)} %get-tuple-element.91.near.refs_2_, bf16[768,128]{1,0:T(8,128)(2,1)} %get-tuple-element.92.refs_3_, ...), custom_call_target="tpu_custom_call" | custom-call | flops 603979776 | bytes 13704192 | tf_op jit(solution)/shard_map/pallas_call | solution.py:570
  135.2 4.3 %all-to-all-done.4.every = bf16[64,24,128]{2,1,0:T(8,128)(2,1)} async-done(((bf16[64,24,128]{2,1,0:T(8,128)(2,1)}), bf16[64,24,128]{2,1,0:T(8,128)(2,1)}, u32[]{:S(2)}, u32[]{:S(2)}) %all-to-all-start.4) | async-done | bytes 393248 | tf_op jit(solution)/shard_map/all_to_all | solution.py:701
  139.5 2.1 %shard_map.132 = (bf16[128,128]{1,0:T(8,128)(2,1)}, f32[128,2,128]{2,1,0:T(2,128)}) custom-call(bf16[64,24,128]{2,1,0:T(8,128)(2,1)} %all-to-all-done.4.every, bf16[48,1536]{1,0:T(8,128)(2,1)} %get-tuple-element.63.coarse, bf16[48,128]{1,0:T(8,128)(2,1)} %get-tuple-element.64.forms, f32[64,128]{1,0:T(8,128)} %get-tuple-element.93.stats), custom_call_target="tpu_custom_call" | custom-call | flops 18874368 | bytes 749568 | tf_op jit(solution)/shard_map/pallas_call | solution.py:570
  141.6 6.5 %all-to-all-start.5 = ((f32[128,2,128]{2,1,0:T(2,128)}), f32[128,2,128]{2,1,0:T(2,128)}, u32[]{:S(2)}, u32[]{:S(2)}) async-start(f32[128,2,128]{2,1,0:T(2,128)} %get-tuple-element.94), calls=%async_computation.5 | async-start | bytes 262144 | tf_op jit(solution)/shard_map/all_to_all | solution.py:743
  148.2 2.4 %shard_map.133 = (f32[768,128]{1,0:T(8,128)}, f32[768,128]{1,0:T(8,128)}) custom-call(bf16[128,128]{1,0:T(8,128)(2,1)} %get-tuple-element.96.stack, f32[768,128]{1,0:T(8,128)} %get-tuple-element.97.g, f32[768,128]{1,0:T(8,128)} %get-tuple-element.98.gp, bf16[768,128]{1,0:T(8,128)(2,1)} %get-tuple-element.57.md, bf16[768,128]{1,0:T(8,128)(2,1)} %get-tuple-element.75.md_p), custom_call_target="tpu_custom_call" | custom-call | flops 50331648 | bytes 1998848 | tf_op jit(solution)/shard_map/pallas_call | solution.py:570
  150.6 7.5 %all-to-all-done.5.refs_2_ = f32[128,2,128]{2,1,0:T(2,128)} async-done(((f32[128,2,128]{2,1,0:T(2,128)}), f32[128,2,128]{2,1,0:T(2,128)}, u32[]{:S(2)}, u32[]{:S(2)}) %all-to-all-start.5) | async-done | bytes 131104 | tf_op jit(solution)/shard_map/all_to_all | solution.py:743
  158.1 4.2 %shard_map.134 = (f32[768,128]{1,0:T(8,128)}, bf16[768,128]{1,0:T(8,128)(2,1)}, bf16[768,128]{1,0:T(8,128)(2,1)}, bf16[768,128]{1,0:T(8,128)(2,1)}, f32[24,128]{1,0:T(8,128)}) custom-call(f32[1,768]{1,0:T(1,128)} %weights.3, f32[8,768]{1,0:T(8,128)} %get-tuple-element.61.refs_1_, f32[128,2,128]{2,1,0:T(2,128)} %all-to-all-done.5.refs_2_, ...), custom_call_target="tpu_custom_call" | custom-call | flops 603979776 | bytes 15260672 | tf_op jit(solution)/shard_map/pallas_call | solution.py:570
  162.8 4.4 %shard_map.135.slave = f32[768,128]{1,0:T(8,128)} custom-call(bf16[768,128]{1,0:T(8,128)(2,1)} %get-tuple-element.103.load_m, bf16[768,128]{1,0:T(8,128)(2,1)} %get-tuple-element.104.load_s, f32[1,768]{1,0:T(1,128)} %weights.3, f32[1536,128]{1,0:T(8,128)} %shard_map.114.refs_7_.refs_9_.fixed, bf16[2304,2304]{1,0:T(8,128)(2,1)} %bitcast.15), custom_call_target="tpu_custom_call" | custom-call | flops 99999997952 | bytes 12192768 | tf_op jit(solution)/shard_map/pallas_call | solution.py:570
  167.8 2.2 %shard_map.136 = f32[768,128]{1,0:T(8,128)} custom-call(f32[768,128]{1,0:T(8,128)} %shard_map.135.slave, bf16[768,128]{1,0:T(8,128)(2,1)} %collective-permute-done.12.um_n, bf16[1152,128]{1,0:T(8,128)(2,1)} %get-tuple-element.68.refs_8_.tiles_s), custom_call_target="tpu_custom_call" | custom-call | flops 37748736 | bytes 1277952 | tf_op jit(solution)/shard_map/pallas_call | solution.py:570
  (30 shorter events, 15.0 us)
Async XLA Ops:
  3.4 9.2 %collective-permute-start = (bf16[2112,128]{1,0:T(8,128)(2,1)}, bf16[2112,128]{1,0:T(8,128)(2,1)}, u32[]{:S(2)}, u32[]{:S(2)}) collective-permute-start(bf16[2112,128]{1,0:T(8,128)(2,1)} %get-tuple-element.54.refs_4_), channel_id=1, source_target_pairs={{124,0},{0,4},{4,8},{8,12},{12,16},{16,20},{20,24},{24,28},{28,32}... | collective-permute-start | bytes 1622024 | tf_op jit(solution)/shard_map/ppermute | solution.py:22
  6.0 6.5 %collective-permute-start.1 = (f32[16,768]{1,0:T(8,128)}, f32[16,768]{1,0:T(8,128)}, u32[]{:S(2)}, u32[]{:S(2)}) collective-permute-start(f32[16,768]{1,0:T(8,128)} %get-tuple-element.55), channel_id=1, source_target_pairs={{4,0},{8,4},{12,8},{16,12},{20,16},{24,20},{28,24},{32,28},{36,32}... | collective-permute-start | bytes 147464 | tf_op jit(solution)/shard_map/ppermute | solution.py:22
  6.0 54.4 %collective-permute-start.5 = (f32[768,128]{1,0:T(8,128)}, f32[768,128]{1,0:T(8,128)}, u32[]{:S(2)}, u32[]{:S(2)}) collective-permute-start(f32[768,128]{1,0:T(8,128)} %bitcast.22), channel_id=1, source_target_pairs={{124,0},{0,4},{4,8},{8,12},{12,16},{16,20},{20,24},{24,28},{28,32}... | collective-permute-start | bytes 1179656 | tf_op jit(solution)/shard_map/ppermute | solution.py:22
  20.1 5.9 %collective-permute-start.2 = (f32[24,128]{1,0:T(8,128)}, f32[24,128]{1,0:T(8,128)}, u32[]{:S(2)}, u32[]{:S(2)}) collective-permute-start(f32[24,128]{1,0:T(8,128)} %get-tuple-element.62.resid), channel_id=1, source_target_pairs={{4,0},{0,4},{12,8},{8,12},{20,16},{16,20},{28,24},{24,28},{36,32},... | collective-permute-start | bytes 36872 | tf_op jit(solution)/shard_map/ppermute | solution.py:27
  25.4 15.5 %collective-permute-start.3 = (bf16[768,128]{1,0:T(8,128)(2,1)}, bf16[768,128]{1,0:T(8,128)(2,1)}, u32[]{:S(2)}, u32[]{:S(2)}) collective-permute-start(bf16[768,128]{1,0:T(8,128)(2,1)} %get-tuple-element.60.near.refs_2_), channel_id=1, source_target_pairs={{4,0},{0,4},{12,8},{8,12},{20,16},{16,20},{28,24},{24,28},{36,32},... | collective-permute-start | bytes 589832 | tf_op jit(solution)/shard_map/ppermute | solution.py:27
  25.4 15.5 %collective-permute-start.4 = (bf16[768,128]{1,0:T(8,128)(2,1)}, bf16[768,128]{1,0:T(8,128)(2,1)}, u32[]{:S(2)}, u32[]{:S(2)}) collective-permute-start(bf16[768,128]{1,0:T(8,128)(2,1)} %get-tuple-element.65.refs_3_), channel_id=1, source_target_pairs={{124,0},{8,4},{4,8},{16,12},{12,16},{24,20},{20,24},{32,28},{28,32... | collective-permute-start | bytes 589832 | tf_op jit(solution)/shard_map/ppermute | solution.py:33
  27.5 21.8 %all-to-all-start = ((bf16[64,24,128]{2,1,0:T(8,128)(2,1)}), bf16[64,24,128]{2,1,0:T(8,128)(2,1)}, u32[]{:S(2)}, u32[]{:S(2)}) async-start(bf16[64,24,128]{2,1,0:T(8,128)(2,1)} %shard_map.117), calls=%async_computation | async-start | bytes 786432 | tf_op jit(solution)/shard_map/all_to_all | solution.py:701
  51.4 16.4 %all-to-all-start.1 = ((f32[128,2,128]{2,1,0:T(2,128)}), f32[128,2,128]{2,1,0:T(2,128)}, u32[]{:S(2)}, u32[]{:S(2)}) async-start(f32[128,2,128]{2,1,0:T(2,128)} %get-tuple-element.71), calls=%async_computation.1 | async-start | bytes 262144 | tf_op jit(solution)/shard_map/all_to_all | solution.py:743
  73.3 2.6 %collective-permute-start.6 = (f32[24,128]{1,0:T(8,128)}, f32[24,128]{1,0:T(8,128)}, u32[]{:S(2)}, u32[]{:S(2)}) collective-permute-start(f32[24,128]{1,0:T(8,128)} %get-tuple-element.78.resid), channel_id=1, source_target_pairs={{4,0},{0,4},{12,8},{8,12},{20,16},{16,20},{28,24},{24,28},{36,32},... | collective-permute-start | bytes 36872 | tf_op jit(solution)/shard_map/ppermute | solution.py:27
  73.8 10.4 %collective-permute-start.8 = (bf16[768,128]{1,0:T(8,128)(2,1)}, bf16[768,128]{1,0:T(8,128)(2,1)}, u32[]{:S(2)}, u32[]{:S(2)}) collective-permute-start(bf16[768,128]{1,0:T(8,128)(2,1)} %get-tuple-element.80.refs_3_), channel_id=1, source_target_pairs={{124,0},{8,4},{4,8},{16,12},{12,16},{24,20},{20,24},{32,28},{28,32... | collective-permute-start | bytes 589832 | tf_op jit(solution)/shard_map/ppermute | solution.py:33
  74.1 10.1 %collective-permute-start.7 = (bf16[768,128]{1,0:T(8,128)(2,1)}, bf16[768,128]{1,0:T(8,128)(2,1)}, u32[]{:S(2)}, u32[]{:S(2)}) collective-permute-start(bf16[768,128]{1,0:T(8,128)(2,1)} %get-tuple-element.79.near.refs_2_), channel_id=1, source_target_pairs={{4,0},{0,4},{12,8},{8,12},{20,16},{16,20},{28,24},{24,28},{36,32},... | collective-permute-start | bytes 589832 | tf_op jit(solution)/shard_map/ppermute | solution.py:27
  77.4 16.8 %all-to-all-start.2 = ((bf16[64,24,128]{2,1,0:T(8,128)(2,1)}), bf16[64,24,128]{2,1,0:T(8,128)(2,1)}, u32[]{:S(2)}, u32[]{:S(2)}) async-start(bf16[64,24,128]{2,1,0:T(8,128)(2,1)} %shard_map.123), calls=%async_computation.2 | async-start | bytes 786432 | tf_op jit(solution)/shard_map/all_to_all | solution.py:701
  96.3 16.4 %all-to-all-start.3 = ((f32[128,2,128]{2,1,0:T(2,128)}), f32[128,2,128]{2,1,0:T(2,128)}, u32[]{:S(2)}, u32[]{:S(2)}) async-start(f32[128,2,128]{2,1,0:T(2,128)} %get-tuple-element.82), calls=%async_computation.3 | async-start | bytes 262144 | tf_op jit(solution)/shard_map/all_to_all | solution.py:743
  118.4 2.6 %collective-permute-start.9 = (f32[24,128]{1,0:T(8,128)}, f32[24,128]{1,0:T(8,128)}, u32[]{:S(2)}, u32[]{:S(2)}) collective-permute-start(f32[24,128]{1,0:T(8,128)} %get-tuple-element.90.resid), channel_id=1, source_target_pairs={{4,0},{0,4},{12,8},{8,12},{20,16},{16,20},{28,24},{24,28},{36,32},... | collective-permute-start | bytes 36872 | tf_op jit(solution)/shard_map/ppermute | solution.py:27
  118.9 10.6 %collective-permute-start.11 = (bf16[768,128]{1,0:T(8,128)(2,1)}, bf16[768,128]{1,0:T(8,128)(2,1)}, u32[]{:S(2)}, u32[]{:S(2)}) collective-permute-start(bf16[768,128]{1,0:T(8,128)(2,1)} %get-tuple-element.92.refs_3_), channel_id=1, source_target_pairs={{124,0},{8,4},{4,8},{16,12},{12,16},{24,20},{20,24},{32,28},{28,32... | collective-permute-start | bytes 589832 | tf_op jit(solution)/shard_map/ppermute | solution.py:33
  119.4 10.1 %collective-permute-start.10 = (bf16[768,128]{1,0:T(8,128)(2,1)}, bf16[768,128]{1,0:T(8,128)(2,1)}, u32[]{:S(2)}, u32[]{:S(2)}) collective-permute-start(bf16[768,128]{1,0:T(8,128)(2,1)} %get-tuple-element.91.near.refs_2_), channel_id=1, source_target_pairs={{4,0},{0,4},{12,8},{8,12},{20,16},{16,20},{28,24},{24,28},{36,32},... | collective-permute-start | bytes 589832 | tf_op jit(solution)/shard_map/ppermute | solution.py:27
  122.4 17.1 %all-to-all-start.4 = ((bf16[64,24,128]{2,1,0:T(8,128)(2,1)}), bf16[64,24,128]{2,1,0:T(8,128)(2,1)}, u32[]{:S(2)}, u32[]{:S(2)}) async-start(bf16[64,24,128]{2,1,0:T(8,128)(2,1)} %shard_map.129), calls=%async_computation.4 | async-start | bytes 786432 | tf_op jit(solution)/shard_map/all_to_all | solution.py:701
  141.6 16.5 %all-to-all-start.5 = ((f32[128,2,128]{2,1,0:T(2,128)}), f32[128,2,128]{2,1,0:T(2,128)}, u32[]{:S(2)}, u32[]{:S(2)}) async-start(f32[128,2,128]{2,1,0:T(2,128)} %get-tuple-element.94), calls=%async_computation.5 | async-start | bytes 262144 | tf_op jit(solution)/shard_map/all_to_all | solution.py:743
  162.3 5.5 %collective-permute-start.12 = (bf16[768,128]{1,0:T(8,128)(2,1)}, bf16[768,128]{1,0:T(8,128)(2,1)}, u32[]{:S(2)}, u32[]{:S(2)}) collective-permute-start(bf16[768,128]{1,0:T(8,128)(2,1)} %get-tuple-element.105), channel_id=1, source_target_pairs={{4,0},{8,4},{12,8},{16,12},{20,16},{24,20},{28,24},{32,28},{36,32}... | collective-permute-start | bytes 589832 | tf_op jit(solution)/shard_map/ppermute | solution.py:22
where the time goes:
time: 171 us; the launch traced here: 170 us
  Pallas kernels  76.6 us (45%)
  starting transfers between devices  57.6 us (34%)
  waiting for transfers between devices  35 us (20%)
    pallas_call x24, Pallas kernels, kernel_call(): pl.pallas_call(body, out_shape=tuple(outs), in_specs=[far if n in anywher...  76.6 us
    all_to_all x3, starting transfers between devices, on_device(): lax.all_to_all(pieces, AXES, 0, 0, tiled=True, axis_index_groups=same_core)  23.3 us
    all_to_all x3, waiting for transfers between devices, on_device(): totals = lax.all_to_all(sums, AXES, 0, 0, tiled=True)  22.5 us
    all_to_all x3, starting transfers between devices, on_device(): totals = lax.all_to_all(sums, AXES, 0, 0, tiled=True)  19.6 us
    all_to_all x3, waiting for transfers between devices, on_device(): lax.all_to_all(pieces, AXES, 0, 0, tiled=True, axis_index_groups=same_core)  11.2 us
    ppermute x6, starting transfers between devices, swapped(): return lax.ppermute(block, 'sub', [(i ^ 1, i) for i in range(size)])  9.04 us
    ppermute x4, starting transfers between devices, shifted(): lax.ppermute(block, 'sub', [((i - distance) % size, i) for i in range(siz...  4.82 us
  transfers between devices with their start and end apart: 19, of which 9 were waited for; matrix products, arithmetic and copies ran while one was open for 0% of the time, Pallas kernels for 31%

commit v1 on v0

--- a/solution.py
+++ b/solution.py
@@ -111,7 +111,7 @@
 
 
 CHUNK = 256
-SIDE = 32
+SIDE = 16
 
 
 def start_faces(moves, kinv, held, ms, first=0, end=None):
@@ -189,8 +189,8 @@
             chosen = cand[:, own].astype(F32)
         lanes = slice(ms + TILE * t, ms + TILE * (t + 1))
         pad = jnp.zeros((8 - nr, TILE), F32)
-        rows = [rigid[:, lanes], pad, coarse[:, own], pad, weights[:, own], chosen]
-        value = jnp.concatenate(rows + [jnp.zeros((SIDE - 18, TILE), F32)], axis=0)
+        rows = [rigid[:, lanes], weights[:, own], chosen, coarse[:, own], pad]
+        value = jnp.concatenate(rows, axis=0)
         high, low = halves(value)
         base = 160 * count + ms + 2 * SIDE * t
         out[base : base + SIDE, :] = high.astype(BF16)
@@ -279,7 +279,7 @@
     modes_p[...] = jnp.zeros_like(modes_p)
     modes[nr : 2 * nr, :] = rigid[:, ms:] * weights[...]
     modes[2 * nr : 3 * nr, :] = -through(tiles_s, side_n[0:nr, :])
-    modes_p[0:nr, :] = side_p[0:nr, :] * side_p[16:17, :]
+    modes_p[0:nr, :] = side_p[0:nr, :] * side_p[6:7, :]
     modes_p[nr : 2 * nr, :] = -through(tiles_p, rigid[:, :ms])
 
     def placed(values):
@@ -362,7 +362,7 @@
         )
 
     floors[...] = jnp.zeros_like(floors)
-    chosen = (cand[...].astype(F32), side_p[17:18, : cand.shape[1]])
+    chosen = (cand[...].astype(F32), side_p[7:8, : cand.shape[1]])
     for t in range(floors.shape[1] // TILE):
         place = lax.broadcasted_iota(jnp.int32, (TILE, cand.shape[1]), 0) + TILE * t
         for n, which in enumerate(chosen):
@@ -437,7 +437,7 @@
     um_n = jnp.where(odd, far_r[...], near_r[...])
     us_p = jnp.where(odd, near_r[...], far_r[...])
     wcol = column(weights[...])
-    gp[...] = column(side_p[16:17, :]) * us_p.astype(F32) - mortar_times(tiles_p, um)
+    gp[...] = column(side_p[6:7, :]) * us_p.astype(F32) - mortar_times(tiles_p, um)
     out_p = moves.start(gp, gp_out)
     wait(7)
     master = (-mortar_t_times(tiles_pt, gp[...].astype(BF16))).astype(BF16)

time: 171 us -> 170 us (level)
  transfers between devices with their start and end apart: 19 -> 19, of which waited for: 9 -> 8; matrix products, arithmetic and copies ran while one was open for 0% -> 0% of each run, Pallas kernels for 31% -> 31%
where the time goes in v1:
time: 170 us; the launch traced here: 169 us
  Pallas kernels  76.4 us (45%)
  starting transfers between devices  56.5 us (33%)
  waiting for transfers between devices  35.6 us (21%)
    pallas_call x24, Pallas kernels, kernel_call(): pl.pallas_call(body, out_shape=tuple(outs), in_specs=[far if n in anywher...  76.4 us
    all_to_all x3, starting transfers between devices, on_device(): lax.all_to_all(pieces, AXES, 0, 0, tiled=True, axis_index_groups=same_core)  23.5 us
    all_to_all x3, waiting for transfers between devices, on_device(): totals = lax.all_to_all(sums, AXES, 0, 0, tiled=True)  22.5 us
    all_to_all x3, starting transfers between devices, on_device(): totals = lax.all_to_all(sums, AXES, 0, 0, tiled=True)  19 us
    all_to_all x3, waiting for transfers between devices, on_device(): lax.all_to_all(pieces, AXES, 0, 0, tiled=True, axis_index_groups=same_core)  11.8 us
    ppermute x6, starting transfers between devices, swapped(): return lax.ppermute(block, 'sub', [(i ^ 1, i) for i in range(size)])  8.51 us
    ppermute x4, starting transfers between devices, shifted(): lax.ppermute(block, 'sub', [((i - distance) % size, i) for i in range(siz...  4.8 us
  transfers between devices with their start and end apart: 19, of which 8 were waited for; matrix products, arithmetic and copies ran while one was open for 0% of the time, Pallas kernels for 31%

profile of v1, /device:TPU:1, one launch (start us, length us, event | category | flops | bytes accessed | tf_op | source)
XLA Modules:
  0.0 169.3 jit_solution(13123305609502278524)
XLA Ops:
  0.6 2.7 %shard_map.113 = (bf16[1920,128]{1,0:T(8,128)(2,1)}, f32[16,768]{1,0:T(8,128)}) custom-call(bf16[768,768]{1,0:T(8,128)(2,1)} %bitcast.25, s32[1,768]{1,0:T(1,128)} %seg.1, f32[768,128]{1,0:T(8,128)} %bitcast.21, f32[1,9216]{1,0:T(1,128)} %bitcast.27, f32[6,768]{1,0:T(8,128)} %coarse.3, f32[1,768]{1,0:T(1,128)} %weights.3, s32[1,384]{1,0:T(1,128)} %cand.3), custom_call_target="tpu_custom_call" | custom-call | bytes 2176512 | tf_op jit(solution)/shard_map/pallas_call | solution.py:570
  3.4 2.6 %collective-permute-start = (bf16[1920,128]{1,0:T(8,128)(2,1)}, bf16[1920,128]{1,0:T(8,128)(2,1)}, u32[]{:S(2)}, u32[]{:S(2)}) collective-permute-start(bf16[1920,128]{1,0:T(8,128)(2,1)} %get-tuple-element.54.refs_4_), channel_id=1, source_target_pairs={{124,0},{0,4},{4,8},{8,12},{12,16},{16,20},{20,24},{24,28},{28,32}... | collective-permute-start | bytes 1474568 | tf_op jit(solution)/shard_map/ppermute | solution.py:22
  7.7 4.7 %shard_map.114.refs_7_.refs_9_.fixed = f32[1536,128]{1,0:T(8,128)} custom-call(bf16[2304,128]{1,0:T(8,128)(2,1)} %bitcast.16, bf16[2304,2304]{1,0:T(8,128)(2,1)} %bitcast.7), custom_call_target="tpu_custom_call" | custom-call | flops 301989888 | bytes 11993088 | tf_op jit(solution)/shard_map/pallas_call | solution.py:570
  12.5 7.5 %shard_map.115 = (bf16[1152,128]{1,0:T(8,128)(2,1)}, bf16[1152,128]{1,0:T(8,128)(2,1)}, bf16[768,256]{1,0:T(8,128)(2,1)}, f32[16,768]{1,0:T(8,128)}, bf16[48,153...) custom-call(bf16[1920,128]{1,0:T(8,128)(2,1)} %collective-permute-do, ...), custom_call_target="tpu_custom_call" | custom-call | flops 603979776 | bytes 15584256 | tf_op jit(solution)/shard_map/pallas_call | solution.py:570
  19.9 4.3 %collective-permute-start.2 = (f32[24,128]{1,0:T(8,128)}, f32[24,128]{1,0:T(8,128)}, u32[]{:S(2)}, u32[]{:S(2)}) collective-permute-start(f32[24,128]{1,0:T(8,128)} %get-tuple-element.62.resid), channel_id=1, source_target_pairs={{4,0},{0,4},{12,8},{8,12},{20,16},{16,20},{28,24},{24,28},{36,32},... | collective-permute-start | bytes 36872 | tf_op jit(solution)/shard_map/ppermute | solution.py:27
  26.9 10.7 %all-to-all-start = ((bf16[64,24,128]{2,1,0:T(8,128)(2,1)}), bf16[64,24,128]{2,1,0:T(8,128)(2,1)}, u32[]{:S(2)}, u32[]{:S(2)}) async-start(bf16[64,24,128]{2,1,0:T(8,128)(2,1)} %shard_map.117), calls=%async_computation | async-start | bytes 786432 | tf_op jit(solution)/shard_map/all_to_all | solution.py:701
  37.6 2.6 %shard_map.116 = (bf16[64,768]{1,0:T(8,128)(2,1)}, bf16[48,128]{1,0:T(8,128)(2,1)}, bf16[48,1536]{1,0:T(8,128)(2,1)}, f32[8,768]{1,0:T(8,128)}) custom-call(bf16[48,1536]{1,0:T(8,128)(2,1)} %get-tuple-element.56.zt.refs_10_.refs_8_, bf16[768,128]{1,0:T(8,128)(2,1)} %get-tuple-element.57.md, bf16[48,1536]{1,0:T(8,128)(2,1)} %get-tuple-element.58.klt.refs_11_, ...), custom_call_target="tpu_custom_call" | custom-call | flops 99999997952 | bytes 1095168 | tf_op jit(solution)/shard_map/pallas_call | solution.py:570
  40.3 5.7 %shard_map.119 = (f32[768,128]{1,0:T(8,128)}, f32[768,128]{1,0:T(8,128)}, f32[64,128]{1,0:T(8,128)}) custom-call(f32[1,768]{1,0:T(1,128)} %weights.3, f32[16,768]{1,0:T(8,128)} %get-tuple-element.59.side_p.refs_1_, bf16[768,128]{1,0:T(8,128)(2,1)} %get-tuple-element.60.near.refs_2_, bf16[768,128]{1,0:T(8,128)(2,1)} %get-tuple-element.65.refs_3_, ...), custom_call_target="tpu_custom_call" | custom-call | flops 603979776 | bytes 13655040 | tf_op jit(solution)/shard_map/pallas_call | solution.py:570
  46.0 3.2 %all-to-all-done.every = bf16[64,24,128]{2,1,0:T(8,128)(2,1)} async-done(((bf16[64,24,128]{2,1,0:T(8,128)(2,1)}), bf16[64,24,128]{2,1,0:T(8,128)(2,1)}, u32[]{:S(2)}, u32[]{:S(2)}) %all-to-all-start) | async-done | bytes 393248 | tf_op jit(solution)/shard_map/all_to_all | solution.py:701
  49.2 2.1 %shard_map.120 = (bf16[128,128]{1,0:T(8,128)(2,1)}, f32[128,2,128]{2,1,0:T(2,128)}) custom-call(bf16[64,24,128]{2,1,0:T(8,128)(2,1)} %all-to-all-done.every, bf16[48,1536]{1,0:T(8,128)(2,1)} %get-tuple-element.63.coarse, bf16[48,128]{1,0:T(8,128)(2,1)} %get-tuple-element.64.forms, f32[64,128]{1,0:T(8,128)} %get-tuple-element.70.stats), custom_call_target="tpu_custom_call" | custom-call | flops 18874368 | bytes 749568 | tf_op jit(solution)/shard_map/pallas_call | solution.py:570
  51.3 6.0 %all-to-all-start.1 = ((f32[128,2,128]{2,1,0:T(2,128)}), f32[128,2,128]{2,1,0:T(2,128)}, u32[]{:S(2)}, u32[]{:S(2)}) async-start(f32[128,2,128]{2,1,0:T(2,128)} %get-tuple-element.71), calls=%async_computation.1 | async-start | bytes 262144 | tf_op jit(solution)/shard_map/all_to_all | solution.py:743
  57.3 2.4 %shard_map.121 = (f32[768,128]{1,0:T(8,128)}, f32[768,128]{1,0:T(8,128)}) custom-call(bf16[128,128]{1,0:T(8,128)(2,1)} %get-tuple-element.72.stack, f32[768,128]{1,0:T(8,128)} %get-tuple-element.73.g, f32[768,128]{1,0:T(8,128)} %get-tuple-element.74.gp, bf16[768,128]{1,0:T(8,128)(2,1)} %get-tuple-element.57.md, bf16[768,128]{1,0:T(8,128)(2,1)} %get-tuple-element.75.md_p), custom_call_target="tpu_custom_call" | custom-call | flops 50331648 | bytes 1998848 | tf_op jit(solution)/shard_map/pallas_call | solution.py:570
  59.7 7.4 %all-to-all-done.1.refs_2_ = f32[128,2,128]{2,1,0:T(2,128)} async-done(((f32[128,2,128]{2,1,0:T(2,128)}), f32[128,2,128]{2,1,0:T(2,128)}, u32[]{:S(2)}, u32[]{:S(2)}) %all-to-all-start.1) | async-done | bytes 131104 | tf_op jit(solution)/shard_map/all_to_all | solution.py:743
  67.1 5.6 %shard_map.122 = (f32[768,128]{1,0:T(8,128)}, f32[768,128]{1,0:T(8,128)}, bf16[768,128]{1,0:T(8,128)(2,1)}, bf16[768,128]{1,0:T(8,128)(2,1)}, f32[24,128]{1,0:T(8,128)}) custom-call(f32[1,768]{1,0:T(1,128)} %weights.3, f32[8,768]{1,0:T(8,128)} %get-tuple-element.61.refs_1_, f32[128,2,128]{2,1,0:T(2,128)} %all-to-all-done.1.refs_2_, ...), custom_call_target="tpu_custom_call" | custom-call | flops 603979776 | bytes 15457280 | tf_op jit(solution)/shard_map/pallas_call | solution.py:570
  76.6 6.3 %all-to-all-start.2 = ((bf16[64,24,128]{2,1,0:T(8,128)(2,1)}), bf16[64,24,128]{2,1,0:T(8,128)(2,1)}, u32[]{:S(2)}, u32[]{:S(2)}) async-start(bf16[64,24,128]{2,1,0:T(8,128)(2,1)} %shard_map.123), calls=%async_computation.2 | async-start | bytes 786432 | tf_op jit(solution)/shard_map/all_to_all | solution.py:701
  83.5 5.7 %shard_map.125 = (f32[768,128]{1,0:T(8,128)}, f32[768,128]{1,0:T(8,128)}, f32[64,128]{1,0:T(8,128)}) custom-call(f32[1,768]{1,0:T(1,128)} %weights.3, f32[16,768]{1,0:T(8,128)} %get-tuple-element.59.side_p.refs_1_, bf16[768,128]{1,0:T(8,128)(2,1)} %get-tuple-element.79.near.refs_2_, bf16[768,128]{1,0:T(8,128)(2,1)} %get-tuple-element.80.refs_3_, ...), custom_call_target="tpu_custom_call" | custom-call | flops 603979776 | bytes 13655040 | tf_op jit(solution)/shard_map/pallas_call | solution.py:570
  89.2 4.3 %all-to-all-done.2.every = bf16[64,24,128]{2,1,0:T(8,128)(2,1)} async-done(((bf16[64,24,128]{2,1,0:T(8,128)(2,1)}), bf16[64,24,128]{2,1,0:T(8,128)(2,1)}, u32[]{:S(2)}, u32[]{:S(2)}) %all-to-all-start.2) | async-done | bytes 393248 | tf_op jit(solution)/shard_map/all_to_all | solution.py:701
  93.6 2.1 %shard_map.126 = (bf16[128,128]{1,0:T(8,128)(2,1)}, f32[128,2,128]{2,1,0:T(2,128)}) custom-call(bf16[64,24,128]{2,1,0:T(8,128)(2,1)} %all-to-all-done.2.every, bf16[48,1536]{1,0:T(8,128)(2,1)} %get-tuple-element.63.coarse, bf16[48,128]{1,0:T(8,128)(2,1)} %get-tuple-element.64.forms, f32[64,128]{1,0:T(8,128)} %get-tuple-element.81.stats), custom_call_target="tpu_custom_call" | custom-call | flops 18874368 | bytes 749568 | tf_op jit(solution)/shard_map/pallas_call | solution.py:570
  95.7 6.5 %all-to-all-start.3 = ((f32[128,2,128]{2,1,0:T(2,128)}), f32[128,2,128]{2,1,0:T(2,128)}, u32[]{:S(2)}, u32[]{:S(2)}) async-start(f32[128,2,128]{2,1,0:T(2,128)} %get-tuple-element.82), calls=%async_computation.3 | async-start | bytes 262144 | tf_op jit(solution)/shard_map/all_to_all | solution.py:743
  102.2 2.4 %shard_map.127 = (f32[768,128]{1,0:T(8,128)}, f32[768,128]{1,0:T(8,128)}) custom-call(bf16[128,128]{1,0:T(8,128)(2,1)} %get-tuple-element.84.stack, f32[768,128]{1,0:T(8,128)} %get-tuple-element.85.g, f32[768,128]{1,0:T(8,128)} %get-tuple-element.86.gp, bf16[768,128]{1,0:T(8,128)(2,1)} %get-tuple-element.57.md, bf16[768,128]{1,0:T(8,128)(2,1)} %get-tuple-element.75.md_p), custom_call_target="tpu_custom_call" | custom-call | flops 50331648 | bytes 1998848 | tf_op jit(solution)/shard_map/pallas_call | solution.py:570
  104.6 7.5 %all-to-all-done.3.refs_2_ = f32[128,2,128]{2,1,0:T(2,128)} async-done(((f32[128,2,128]{2,1,0:T(2,128)}), f32[128,2,128]{2,1,0:T(2,128)}, u32[]{:S(2)}, u32[]{:S(2)}) %all-to-all-start.3) | async-done | bytes 131104 | tf_op jit(solution)/shard_map/all_to_all | solution.py:743
  112.1 5.6 %shard_map.128 = (f32[768,128]{1,0:T(8,128)}, f32[768,128]{1,0:T(8,128)}, bf16[768,128]{1,0:T(8,128)(2,1)}, bf16[768,128]{1,0:T(8,128)(2,1)}, f32[24,128]{1,0:T(8,128)}) custom-call(f32[1,768]{1,0:T(1,128)} %weights.3, f32[8,768]{1,0:T(8,128)} %get-tuple-element.61.refs_1_, f32[128,2,128]{2,1,0:T(2,128)} %all-to-all-done.3.refs_2_, ...), custom_call_target="tpu_custom_call" | custom-call | flops 603979776 | bytes 15457280 | tf_op jit(solution)/shard_map/pallas_call | solution.py:570
  121.8 6.4 %all-to-all-start.4 = ((bf16[64,24,128]{2,1,0:T(8,128)(2,1)}), bf16[64,24,128]{2,1,0:T(8,128)(2,1)}, u32[]{:S(2)}, u32[]{:S(2)}) async-start(bf16[64,24,128]{2,1,0:T(8,128)(2,1)} %shard_map.129), calls=%async_computation.4 | async-start | bytes 786432 | tf_op jit(solution)/shard_map/all_to_all | solution.py:701
  128.8 5.7 %shard_map.131 = (f32[768,128]{1,0:T(8,128)}, f32[768,128]{1,0:T(8,128)}, f32[64,128]{1,0:T(8,128)}) custom-call(f32[1,768]{1,0:T(1,128)} %weights.3, f32[16,768]{1,0:T(8,128)} %get-tuple-element.59.side_p.refs_1_, bf16[768,128]{1,0:T(8,128)(2,1)} %get-tuple-element.91.near.refs_2_, bf16[768,128]{1,0:T(8,128)(2,1)} %get-tuple-element.92.refs_3_, ...), custom_call_target="tpu_custom_call" | custom-call | flops 603979776 | bytes 13655040 | tf_op jit(solution)/shard_map/pallas_call | solution.py:570
  134.5 4.3 %all-to-all-done.4.every = bf16[64,24,128]{2,1,0:T(8,128)(2,1)} async-done(((bf16[64,24,128]{2,1,0:T(8,128)(2,1)}), bf16[64,24,128]{2,1,0:T(8,128)(2,1)}, u32[]{:S(2)}, u32[]{:S(2)}) %all-to-all-start.4) | async-done | bytes 393248 | tf_op jit(solution)/shard_map/all_to_all | solution.py:701
  138.8 2.1 %shard_map.132 = (bf16[128,128]{1,0:T(8,128)(2,1)}, f32[128,2,128]{2,1,0:T(2,128)}) custom-call(bf16[64,24,128]{2,1,0:T(8,128)(2,1)} %all-to-all-done.4.every, bf16[48,1536]{1,0:T(8,128)(2,1)} %get-tuple-element.63.coarse, bf16[48,128]{1,0:T(8,128)(2,1)} %get-tuple-element.64.forms, f32[64,128]{1,0:T(8,128)} %get-tuple-element.93.stats), custom_call_target="tpu_custom_call" | custom-call | flops 18874368 | bytes 749568 | tf_op jit(solution)/shard_map/pallas_call | solution.py:570
  141.0 6.5 %all-to-all-start.5 = ((f32[128,2,128]{2,1,0:T(2,128)}), f32[128,2,128]{2,1,0:T(2,128)}, u32[]{:S(2)}, u32[]{:S(2)}) async-start(f32[128,2,128]{2,1,0:T(2,128)} %get-tuple-element.94), calls=%async_computation.5 | async-start | bytes 262144 | tf_op jit(solution)/shard_map/all_to_all | solution.py:743
  147.5 2.4 %shard_map.133 = (f32[768,128]{1,0:T(8,128)}, f32[768,128]{1,0:T(8,128)}) custom-call(bf16[128,128]{1,0:T(8,128)(2,1)} %get-tuple-element.96.stack, f32[768,128]{1,0:T(8,128)} %get-tuple-element.97.g, f32[768,128]{1,0:T(8,128)} %get-tuple-element.98.gp, bf16[768,128]{1,0:T(8,128)(2,1)} %get-tuple-element.57.md, bf16[768,128]{1,0:T(8,128)(2,1)} %get-tuple-element.75.md_p), custom_call_target="tpu_custom_call" | custom-call | flops 50331648 | bytes 1998848 | tf_op jit(solution)/shard_map/pallas_call | solution.py:570
  149.9 7.5 %all-to-all-done.5.refs_2_ = f32[128,2,128]{2,1,0:T(2,128)} async-done(((f32[128,2,128]{2,1,0:T(2,128)}), f32[128,2,128]{2,1,0:T(2,128)}, u32[]{:S(2)}, u32[]{:S(2)}) %all-to-all-start.5) | async-done | bytes 131104 | tf_op jit(solution)/shard_map/all_to_all | solution.py:743
  157.4 4.2 %shard_map.134 = (f32[768,128]{1,0:T(8,128)}, bf16[768,128]{1,0:T(8,128)(2,1)}, bf16[768,128]{1,0:T(8,128)(2,1)}, bf16[768,128]{1,0:T(8,128)(2,1)}, f32[24,128]{1,0:T(8,128)}) custom-call(f32[1,768]{1,0:T(1,128)} %weights.3, f32[8,768]{1,0:T(8,128)} %get-tuple-element.61.refs_1_, f32[128,2,128]{2,1,0:T(2,128)} %all-to-all-done.5.refs_2_, ...), custom_call_target="tpu_custom_call" | custom-call | flops 603979776 | bytes 15260672 | tf_op jit(solution)/shard_map/pallas_call | solution.py:570
  162.1 4.4 %shard_map.135.slave = f32[768,128]{1,0:T(8,128)} custom-call(bf16[768,128]{1,0:T(8,128)(2,1)} %get-tuple-element.103.load_m, bf16[768,128]{1,0:T(8,128)(2,1)} %get-tuple-element.104.load_s, f32[1,768]{1,0:T(1,128)} %weights.3, f32[1536,128]{1,0:T(8,128)} %shard_map.114.refs_7_.refs_9_.fixed, bf16[2304,2304]{1,0:T(8,128)(2,1)} %bitcast.15), custom_call_target="tpu_custom_call" | custom-call | flops 99999997952 | bytes 12192768 | tf_op jit(solution)/shard_map/pallas_call | solution.py:570
  167.1 2.2 %shard_map.136 = f32[768,128]{1,0:T(8,128)} custom-call(f32[768,128]{1,0:T(8,128)} %shard_map.135.slave, bf16[768,128]{1,0:T(8,128)(2,1)} %collective-permute-done.12.um_n, bf16[1152,128]{1,0:T(8,128)(2,1)} %get-tuple-element.68.refs_8_.tiles_s), custom_call_target="tpu_custom_call" | custom-call | flops 37748736 | bytes 1277952 | tf_op jit(solution)/shard_map/pallas_call | solution.py:570
  (30 shorter events, 14.7 us)
Async XLA Ops:
  3.4 9.1 %collective-permute-start = (bf16[1920,128]{1,0:T(8,128)(2,1)}, bf16[1920,128]{1,0:T(8,128)(2,1)}, u32[]{:S(2)}, u32[]{:S(2)}) collective-permute-start(bf16[1920,128]{1,0:T(8,128)(2,1)} %get-tuple-element.54.refs_4_), channel_id=1, source_target_pairs={{124,0},{0,4},{4,8},{8,12},{12,16},{16,20},{20,24},{24,28},{28,32}... | collective-permute-start | bytes 1474568 | tf_op jit(solution)/shard_map/ppermute | solution.py:22
  6.0 6.5 %collective-permute-start.1 = (f32[16,768]{1,0:T(8,128)}, f32[16,768]{1,0:T(8,128)}, u32[]{:S(2)}, u32[]{:S(2)}) collective-permute-start(f32[16,768]{1,0:T(8,128)} %get-tuple-element.55), channel_id=1, source_target_pairs={{4,0},{8,4},{12,8},{16,12},{20,16},{24,20},{28,24},{32,28},{36,32}... | collective-permute-start | bytes 147464 | tf_op jit(solution)/shard_map/ppermute | solution.py:22
  6.0 53.7 %collective-permute-start.5 = (f32[768,128]{1,0:T(8,128)}, f32[768,128]{1,0:T(8,128)}, u32[]{:S(2)}, u32[]{:S(2)}) collective-permute-start(f32[768,128]{1,0:T(8,128)} %bitcast.22), channel_id=1, source_target_pairs={{124,0},{0,4},{4,8},{8,12},{12,16},{16,20},{20,24},{24,28},{28,32}... | collective-permute-start | bytes 1179656 | tf_op jit(solution)/shard_map/ppermute | solution.py:22
  19.9 5.5 %collective-permute-start.2 = (f32[24,128]{1,0:T(8,128)}, f32[24,128]{1,0:T(8,128)}, u32[]{:S(2)}, u32[]{:S(2)}) collective-permute-start(f32[24,128]{1,0:T(8,128)} %get-tuple-element.62.resid), channel_id=1, source_target_pairs={{4,0},{0,4},{12,8},{8,12},{20,16},{16,20},{28,24},{24,28},{36,32},... | collective-permute-start | bytes 36872 | tf_op jit(solution)/shard_map/ppermute | solution.py:27
  24.8 15.4 %collective-permute-start.3 = (bf16[768,128]{1,0:T(8,128)(2,1)}, bf16[768,128]{1,0:T(8,128)(2,1)}, u32[]{:S(2)}, u32[]{:S(2)}) collective-permute-start(bf16[768,128]{1,0:T(8,128)(2,1)} %get-tuple-element.60.near.refs_2_), channel_id=1, source_target_pairs={{4,0},{0,4},{12,8},{8,12},{20,16},{16,20},{28,24},{24,28},{36,32},... | collective-permute-start | bytes 589832 | tf_op jit(solution)/shard_map/ppermute | solution.py:27
  24.8 15.4 %collective-permute-start.4 = (bf16[768,128]{1,0:T(8,128)(2,1)}, bf16[768,128]{1,0:T(8,128)(2,1)}, u32[]{:S(2)}, u32[]{:S(2)}) collective-permute-start(bf16[768,128]{1,0:T(8,128)(2,1)} %get-tuple-element.65.refs_3_), channel_id=1, source_target_pairs={{124,0},{8,4},{4,8},{16,12},{12,16},{24,20},{20,24},{32,28},{28,32... | collective-permute-start | bytes 589832 | tf_op jit(solution)/shard_map/ppermute | solution.py:33
  26.9 22.3 %all-to-all-start = ((bf16[64,24,128]{2,1,0:T(8,128)(2,1)}), bf16[64,24,128]{2,1,0:T(8,128)(2,1)}, u32[]{:S(2)}, u32[]{:S(2)}) async-start(bf16[64,24,128]{2,1,0:T(8,128)(2,1)} %shard_map.117), calls=%async_computation | async-start | bytes 786432 | tf_op jit(solution)/shard_map/all_to_all | solution.py:701
  51.3 15.8 %all-to-all-start.1 = ((f32[128,2,128]{2,1,0:T(2,128)}), f32[128,2,128]{2,1,0:T(2,128)}, u32[]{:S(2)}, u32[]{:S(2)}) async-start(f32[128,2,128]{2,1,0:T(2,128)} %get-tuple-element.71), calls=%async_computation.1 | async-start | bytes 262144 | tf_op jit(solution)/shard_map/all_to_all | solution.py:743
  72.6 2.4 %collective-permute-start.6 = (f32[24,128]{1,0:T(8,128)}, f32[24,128]{1,0:T(8,128)}, u32[]{:S(2)}, u32[]{:S(2)}) collective-permute-start(f32[24,128]{1,0:T(8,128)} %get-tuple-element.78.resid), channel_id=1, source_target_pairs={{4,0},{0,4},{12,8},{8,12},{20,16},{16,20},{28,24},{24,28},{36,32},... | collective-permute-start | bytes 36872 | tf_op jit(solution)/shard_map/ppermute | solution.py:27
  73.1 10.4 %collective-permute-start.8 = (bf16[768,128]{1,0:T(8,128)(2,1)}, bf16[768,128]{1,0:T(8,128)(2,1)}, u32[]{:S(2)}, u32[]{:S(2)}) collective-permute-start(bf16[768,128]{1,0:T(8,128)(2,1)} %get-tuple-element.80.refs_3_), channel_id=1, source_target_pairs={{124,0},{8,4},{4,8},{16,12},{12,16},{24,20},{20,24},{32,28},{28,32... | collective-permute-start | bytes 589832 | tf_op jit(solution)/shard_map/ppermute | solution.py:33
  73.4 10.1 %collective-permute-start.7 = (bf16[768,128]{1,0:T(8,128)(2,1)}, bf16[768,128]{1,0:T(8,128)(2,1)}, u32[]{:S(2)}, u32[]{:S(2)}) collective-permute-start(bf16[768,128]{1,0:T(8,128)(2,1)} %get-tuple-element.79.near.refs_2_), channel_id=1, source_target_pairs={{4,0},{0,4},{12,8},{8,12},{20,16},{16,20},{28,24},{24,28},{36,32},... | collective-permute-start | bytes 589832 | tf_op jit(solution)/shard_map/ppermute | solution.py:27
  76.6 17.0 %all-to-all-start.2 = ((bf16[64,24,128]{2,1,0:T(8,128)(2,1)}), bf16[64,24,128]{2,1,0:T(8,128)(2,1)}, u32[]{:S(2)}, u32[]{:S(2)}) async-start(bf16[64,24,128]{2,1,0:T(8,128)(2,1)} %shard_map.123), calls=%async_computation.2 | async-start | bytes 786432 | tf_op jit(solution)/shard_map/all_to_all | solution.py:701
  95.7 16.5 %all-to-all-start.3 = ((f32[128,2,128]{2,1,0:T(2,128)}), f32[128,2,128]{2,1,0:T(2,128)}, u32[]{:S(2)}, u32[]{:S(2)}) async-start(f32[128,2,128]{2,1,0:T(2,128)} %get-tuple-element.82), calls=%async_computation.3 | async-start | bytes 262144 | tf_op jit(solution)/shard_map/all_to_all | solution.py:743
  117.7 2.6 %collective-permute-start.9 = (f32[24,128]{1,0:T(8,128)}, f32[24,128]{1,0:T(8,128)}, u32[]{:S(2)}, u32[]{:S(2)}) collective-permute-start(f32[24,128]{1,0:T(8,128)} %get-tuple-element.90.resid), channel_id=1, source_target_pairs={{4,0},{0,4},{12,8},{8,12},{20,16},{16,20},{28,24},{24,28},{36,32},... | collective-permute-start | bytes 36872 | tf_op jit(solution)/shard_map/ppermute | solution.py:27
  118.2 10.6 %collective-permute-start.11 = (bf16[768,128]{1,0:T(8,128)(2,1)}, bf16[768,128]{1,0:T(8,128)(2,1)}, u32[]{:S(2)}, u32[]{:S(2)}) collective-permute-start(bf16[768,128]{1,0:T(8,128)(2,1)} %get-tuple-element.92.refs_3_), channel_id=1, source_target_pairs={{124,0},{8,4},{4,8},{16,12},{12,16},{24,20},{20,24},{32,28},{28,32... | collective-permute-start | bytes 589832 | tf_op jit(solution)/shard_map/ppermute | solution.py:33
  118.7 10.1 %collective-permute-start.10 = (bf16[768,128]{1,0:T(8,128)(2,1)}, bf16[768,128]{1,0:T(8,128)(2,1)}, u32[]{:S(2)}, u32[]{:S(2)}) collective-permute-start(bf16[768,128]{1,0:T(8,128)(2,1)} %get-tuple-element.91.near.refs_2_), channel_id=1, source_target_pairs={{4,0},{0,4},{12,8},{8,12},{20,16},{16,20},{28,24},{24,28},{36,32},... | collective-permute-start | bytes 589832 | tf_op jit(solution)/shard_map/ppermute | solution.py:27
  121.8 17.1 %all-to-all-start.4 = ((bf16[64,24,128]{2,1,0:T(8,128)(2,1)}), bf16[64,24,128]{2,1,0:T(8,128)(2,1)}, u32[]{:S(2)}, u32[]{:S(2)}) async-start(bf16[64,24,128]{2,1,0:T(8,128)(2,1)} %shard_map.129), calls=%async_computation.4 | async-start | bytes 786432 | tf_op jit(solution)/shard_map/all_to_all | solution.py:701
  141.0 16.5 %all-to-all-start.5 = ((f32[128,2,128]{2,1,0:T(2,128)}), f32[128,2,128]{2,1,0:T(2,128)}, u32[]{:S(2)}, u32[]{:S(2)}) async-start(f32[128,2,128]{2,1,0:T(2,128)} %get-tuple-element.94), calls=%async_computation.5 | async-start | bytes 262144 | tf_op jit(solution)/shard_map/all_to_all | solution.py:743
  161.7 5.5 %collective-permute-start.12 = (bf16[768,128]{1,0:T(8,128)(2,1)}, bf16[768,128]{1,0:T(8,128)(2,1)}, u32[]{:S(2)}, u32[]{:S(2)}) collective-permute-start(bf16[768,128]{1,0:T(8,128)(2,1)} %get-tuple-element.105), channel_id=1, source_target_pairs={{4,0},{8,4},{12,8},{16,12},{20,16},{24,20},{28,24},{32,28},{36,32}... | collective-permute-start | bytes 589832 | tf_op jit(solution)/shard_map/ppermute | solution.py:22

commit v2 on v1

--- a/solution.py
+++ b/solution.py
@@ -541,11 +541,13 @@
         solved(copies, held, load, fixed, None, um, us, ms)
         outs += [out_s, moves.start(um, yp_out)]
     else:
-        resid[...] = solved(copies, held, load, fixed, zt, um, us, ms)
+        solved(copies, held, load, fixed, None, um, us, ms)
         odd = is_odd()
         near[...] = jnp.where(odd, um[...], us[...])
         far[...] = jnp.where(odd, us[...], um[...])
         outs = [moves.start(far, far_out), moves.start(near, near_out)]
+        both = dot(zt[:, :ms], um[...]) + dot(zt[:, ms:], us[...])
+        resid[...] = both[:24] + both[24:]
         outs += [out_p, out_s, moves.start(resid, resid_out)]
     for copy in outs:
         copy.wait()

time: 170 us -> 170 us (level)
  no operation moved by 1% of the time
where the time goes in v2:
time: 170 us; the launch traced here: 169 us
  Pallas kernels  76.4 us (45%)
  starting transfers between devices  56.5 us (33%)
  waiting for transfers between devices  35.6 us (21%)
    pallas_call x24, Pallas kernels, kernel_call(): pl.pallas_call(body, out_shape=tuple(outs), in_specs=[far if n in anywher...  76.4 us
    all_to_all x3, starting transfers between devices, on_device(): lax.all_to_all(pieces, AXES, 0, 0, tiled=True, axis_index_groups=same_core)  23.5 us
    all_to_all x3, waiting for transfers between devices, on_device(): totals = lax.all_to_all(sums, AXES, 0, 0, tiled=True)  22.5 us
    all_to_all x3, starting transfers between devices, on_device(): totals = lax.all_to_all(sums, AXES, 0, 0, tiled=True)  19 us
    all_to_all x3, waiting for transfers between devices, on_device(): lax.all_to_all(pieces, AXES, 0, 0, tiled=True, axis_index_groups=same_core)  11.8 us
    ppermute x6, starting transfers between devices, swapped(): return lax.ppermute(block, 'sub', [(i ^ 1, i) for i in range(size)])  8.51 us
    ppermute x4, starting transfers between devices, shifted(): lax.ppermute(block, 'sub', [((i - distance) % size, i) for i in range(siz...  4.8 us
  transfers between devices with their start and end apart: 19, of which 8 were waited for; matrix products, arithmetic and copies ran while one was open for 0% of the time, Pallas kernels for 31%

profile of v2, /device:TPU:1, one launch (start us, length us, event | category | flops | bytes accessed | tf_op | source)
XLA Modules:
  0.0 169.3 jit_solution(13123305609502278524)
XLA Ops:
  0.6 2.7 %shard_map.113 = (bf16[1920,128]{1,0:T(8,128)(2,1)}, f32[16,768]{1,0:T(8,128)}) custom-call(bf16[768,768]{1,0:T(8,128)(2,1)} %bitcast.25, s32[1,768]{1,0:T(1,128)} %seg.1, f32[768,128]{1,0:T(8,128)} %bitcast.21, f32[1,9216]{1,0:T(1,128)} %bitcast.27, f32[6,768]{1,0:T(8,128)} %coarse.3, f32[1,768]{1,0:T(1,128)} %weights.3, s32[1,384]{1,0:T(1,128)} %cand.3), custom_call_target="tpu_custom_call" | custom-call | bytes 2176512 | tf_op jit(solution)/shard_map/pallas_call | solution.py:572
  3.4 2.6 %collective-permute-start = (bf16[1920,128]{1,0:T(8,128)(2,1)}, bf16[1920,128]{1,0:T(8,128)(2,1)}, u32[]{:S(2)}, u32[]{:S(2)}) collective-permute-start(bf16[1920,128]{1,0:T(8,128)(2,1)} %get-tuple-element.54.refs_4_), channel_id=1, source_target_pairs={{124,0},{0,4},{4,8},{8,12},{12,16},{16,20},{20,24},{24,28},{28,32}... | collective-permute-start | bytes 1474568 | tf_op jit(solution)/shard_map/ppermute | solution.py:22
  7.7 4.7 %shard_map.114.refs_7_.refs_9_.fixed = f32[1536,128]{1,0:T(8,128)} custom-call(bf16[2304,128]{1,0:T(8,128)(2,1)} %bitcast.16, bf16[2304,2304]{1,0:T(8,128)(2,1)} %bitcast.7), custom_call_target="tpu_custom_call" | custom-call | flops 301989888 | bytes 11993088 | tf_op jit(solution)/shard_map/pallas_call | solution.py:572
  12.5 7.5 %shard_map.115 = (bf16[1152,128]{1,0:T(8,128)(2,1)}, bf16[1152,128]{1,0:T(8,128)(2,1)}, bf16[768,256]{1,0:T(8,128)(2,1)}, f32[16,768]{1,0:T(8,128)}, bf16[48,153...) custom-call(bf16[1920,128]{1,0:T(8,128)(2,1)} %collective-permute-do, ...), custom_call_target="tpu_custom_call" | custom-call | flops 603979776 | bytes 15584256 | tf_op jit(solution)/shard_map/pallas_call | solution.py:572
  19.9 4.3 %collective-permute-start.2 = (f32[24,128]{1,0:T(8,128)}, f32[24,128]{1,0:T(8,128)}, u32[]{:S(2)}, u32[]{:S(2)}) collective-permute-start(f32[24,128]{1,0:T(8,128)} %get-tuple-element.62.resid), channel_id=1, source_target_pairs={{4,0},{0,4},{12,8},{8,12},{20,16},{16,20},{28,24},{24,28},{36,32},... | collective-permute-start | bytes 36872 | tf_op jit(solution)/shard_map/ppermute | solution.py:27
  26.9 10.7 %all-to-all-start = ((bf16[64,24,128]{2,1,0:T(8,128)(2,1)}), bf16[64,24,128]{2,1,0:T(8,128)(2,1)}, u32[]{:S(2)}, u32[]{:S(2)}) async-start(bf16[64,24,128]{2,1,0:T(8,128)(2,1)} %shard_map.117), calls=%async_computation | async-start | bytes 786432 | tf_op jit(solution)/shard_map/all_to_all | solution.py:703
  37.6 2.6 %shard_map.116 = (bf16[64,768]{1,0:T(8,128)(2,1)}, bf16[48,128]{1,0:T(8,128)(2,1)}, bf16[48,1536]{1,0:T(8,128)(2,1)}, f32[8,768]{1,0:T(8,128)}) custom-call(bf16[48,1536]{1,0:T(8,128)(2,1)} %get-tuple-element.56.zt.refs_10_.refs_8_, bf16[768,128]{1,0:T(8,128)(2,1)} %get-tuple-element.57.md, bf16[48,1536]{1,0:T(8,128)(2,1)} %get-tuple-element.58.klt.refs_11_, ...), custom_call_target="tpu_custom_call" | custom-call | flops 99999997952 | bytes 1095168 | tf_op jit(solution)/shard_map/pallas_call | solution.py:572
  40.3 5.7 %shard_map.119 = (f32[768,128]{1,0:T(8,128)}, f32[768,128]{1,0:T(8,128)}, f32[64,128]{1,0:T(8,128)}) custom-call(f32[1,768]{1,0:T(1,128)} %weights.3, f32[16,768]{1,0:T(8,128)} %get-tuple-element.59.side_p.refs_1_, bf16[768,128]{1,0:T(8,128)(2,1)} %get-tuple-element.60.near.refs_2_, bf16[768,128]{1,0:T(8,128)(2,1)} %get-tuple-element.65.refs_3_, ...), custom_call_target="tpu_custom_call" | custom-call | flops 603979776 | bytes 13655040 | tf_op jit(solution)/shard_map/pallas_call | solution.py:572
  46.0 3.2 %all-to-all-done.every = bf16[64,24,128]{2,1,0:T(8,128)(2,1)} async-done(((bf16[64,24,128]{2,1,0:T(8,128)(2,1)}), bf16[64,24,128]{2,1,0:T(8,128)(2,1)}, u32[]{:S(2)}, u32[]{:S(2)}) %all-to-all-start) | async-done | bytes 393248 | tf_op jit(solution)/shard_map/all_to_all | solution.py:703
  49.2 2.1 %shard_map.120 = (bf16[128,128]{1,0:T(8,128)(2,1)}, f32[128,2,128]{2,1,0:T(2,128)}) custom-call(bf16[64,24,128]{2,1,0:T(8,128)(2,1)} %all-to-all-done.every, bf16[48,1536]{1,0:T(8,128)(2,1)} %get-tuple-element.63.coarse, bf16[48,128]{1,0:T(8,128)(2,1)} %get-tuple-element.64.forms, f32[64,128]{1,0:T(8,128)} %get-tuple-element.70.stats), custom_call_target="tpu_custom_call" | custom-call | flops 18874368 | bytes 749568 | tf_op jit(solution)/shard_map/pallas_call | solution.py:572
  51.3 6.0 %all-to-all-start.1 = ((f32[128,2,128]{2,1,0:T(2,128)}), f32[128,2,128]{2,1,0:T(2,128)}, u32[]{:S(2)}, u32[]{:S(2)}) async-start(f32[128,2,128]{2,1,0:T(2,128)} %get-tuple-element.71), calls=%async_computation.1 | async-start | bytes 262144 | tf_op jit(solution)/shard_map/all_to_all | solution.py:745
  57.3 2.4 %shard_map.121 = (f32[768,128]{1,0:T(8,128)}, f32[768,128]{1,0:T(8,128)}) custom-call(bf16[128,128]{1,0:T(8,128)(2,1)} %get-tuple-element.72.stack, f32[768,128]{1,0:T(8,128)} %get-tuple-element.73.g, f32[768,128]{1,0:T(8,128)} %get-tuple-element.74.gp, bf16[768,128]{1,0:T(8,128)(2,1)} %get-tuple-element.57.md, bf16[768,128]{1,0:T(8,128)(2,1)} %get-tuple-element.75.md_p), custom_call_target="tpu_custom_call" | custom-call | flops 50331648 | bytes 1998848 | tf_op jit(solution)/shard_map/pallas_call | solution.py:572
  59.7 7.4 %all-to-all-done.1.refs_2_ = f32[128,2,128]{2,1,0:T(2,128)} async-done(((f32[128,2,128]{2,1,0:T(2,128)}), f32[128,2,128]{2,1,0:T(2,128)}, u32[]{:S(2)}, u32[]{:S(2)}) %all-to-all-start.1) | async-done | bytes 131104 | tf_op jit(solution)/shard_map/all_to_all | solution.py:745
  67.1 5.6 %shard_map.122 = (f32[768,128]{1,0:T(8,128)}, f32[768,128]{1,0:T(8,128)}, bf16[768,128]{1,0:T(8,128)(2,1)}, bf16[768,128]{1,0:T(8,128)(2,1)}, f32[24,128]{1,0:T(8,128)}) custom-call(f32[1,768]{1,0:T(1,128)} %weights.3, f32[8,768]{1,0:T(8,128)} %get-tuple-element.61.refs_1_, f32[128,2,128]{2,1,0:T(2,128)} %all-to-all-done.1.refs_2_, ...), custom_call_target="tpu_custom_call" | custom-call | flops 603979776 | bytes 15457280 | tf_op jit(solution)/shard_map/pallas_call | solution.py:572
  76.6 6.3 %all-to-all-start.2 = ((bf16[64,24,128]{2,1,0:T(8,128)(2,1)}), bf16[64,24,128]{2,1,0:T(8,128)(2,1)}, u32[]{:S(2)}, u32[]{:S(2)}) async-start(bf16[64,24,128]{2,1,0:T(8,128)(2,1)} %shard_map.123), calls=%async_computation.2 | async-start | bytes 786432 | tf_op jit(solution)/shard_map/all_to_all | solution.py:703
  83.5 5.7 %shard_map.125 = (f32[768,128]{1,0:T(8,128)}, f32[768,128]{1,0:T(8,128)}, f32[64,128]{1,0:T(8,128)}) custom-call(f32[1,768]{1,0:T(1,128)} %weights.3, f32[16,768]{1,0:T(8,128)} %get-tuple-element.59.side_p.refs_1_, bf16[768,128]{1,0:T(8,128)(2,1)} %get-tuple-element.79.near.refs_2_, bf16[768,128]{1,0:T(8,128)(2,1)} %get-tuple-element.80.refs_3_, ...), custom_call_target="tpu_custom_call" | custom-call | flops 603979776 | bytes 13655040 | tf_op jit(solution)/shard_map/pallas_call | solution.py:572
  89.2 4.3 %all-to-all-done.2.every = bf16[64,24,128]{2,1,0:T(8,128)(2,1)} async-done(((bf16[64,24,128]{2,1,0:T(8,128)(2,1)}), bf16[64,24,128]{2,1,0:T(8,128)(2,1)}, u32[]{:S(2)}, u32[]{:S(2)}) %all-to-all-start.2) | async-done | bytes 393248 | tf_op jit(solution)/shard_map/all_to_all | solution.py:703
  93.6 2.1 %shard_map.126 = (bf16[128,128]{1,0:T(8,128)(2,1)}, f32[128,2,128]{2,1,0:T(2,128)}) custom-call(bf16[64,24,128]{2,1,0:T(8,128)(2,1)} %all-to-all-done.2.every, bf16[48,1536]{1,0:T(8,128)(2,1)} %get-tuple-element.63.coarse, bf16[48,128]{1,0:T(8,128)(2,1)} %get-tuple-element.64.forms, f32[64,128]{1,0:T(8,128)} %get-tuple-element.81.stats), custom_call_target="tpu_custom_call" | custom-call | flops 18874368 | bytes 749568 | tf_op jit(solution)/shard_map/pallas_call | solution.py:572
  95.7 6.5 %all-to-all-start.3 = ((f32[128,2,128]{2,1,0:T(2,128)}), f32[128,2,128]{2,1,0:T(2,128)}, u32[]{:S(2)}, u32[]{:S(2)}) async-start(f32[128,2,128]{2,1,0:T(2,128)} %get-tuple-element.82), calls=%async_computation.3 | async-start | bytes 262144 | tf_op jit(solution)/shard_map/all_to_all | solution.py:745
  102.2 2.4 %shard_map.127 = (f32[768,128]{1,0:T(8,128)}, f32[768,128]{1,0:T(8,128)}) custom-call(bf16[128,128]{1,0:T(8,128)(2,1)} %get-tuple-element.84.stack, f32[768,128]{1,0:T(8,128)} %get-tuple-element.85.g, f32[768,128]{1,0:T(8,128)} %get-tuple-element.86.gp, bf16[768,128]{1,0:T(8,128)(2,1)} %get-tuple-element.57.md, bf16[768,128]{1,0:T(8,128)(2,1)} %get-tuple-element.75.md_p), custom_call_target="tpu_custom_call" | custom-call | flops 50331648 | bytes 1998848 | tf_op jit(solution)/shard_map/pallas_call | solution.py:572
  104.6 7.5 %all-to-all-done.3.refs_2_ = f32[128,2,128]{2,1,0:T(2,128)} async-done(((f32[128,2,128]{2,1,0:T(2,128)}), f32[128,2,128]{2,1,0:T(2,128)}, u32[]{:S(2)}, u32[]{:S(2)}) %all-to-all-start.3) | async-done | bytes 131104 | tf_op jit(solution)/shard_map/all_to_all | solution.py:745
  112.1 5.6 %shard_map.128 = (f32[768,128]{1,0:T(8,128)}, f32[768,128]{1,0:T(8,128)}, bf16[768,128]{1,0:T(8,128)(2,1)}, bf16[768,128]{1,0:T(8,128)(2,1)}, f32[24,128]{1,0:T(8,128)}) custom-call(f32[1,768]{1,0:T(1,128)} %weights.3, f32[8,768]{1,0:T(8,128)} %get-tuple-element.61.refs_1_, f32[128,2,128]{2,1,0:T(2,128)} %all-to-all-done.3.refs_2_, ...), custom_call_target="tpu_custom_call" | custom-call | flops 603979776 | bytes 15457280 | tf_op jit(solution)/shard_map/pallas_call | solution.py:572
  121.8 6.4 %all-to-all-start.4 = ((bf16[64,24,128]{2,1,0:T(8,128)(2,1)}), bf16[64,24,128]{2,1,0:T(8,128)(2,1)}, u32[]{:S(2)}, u32[]{:S(2)}) async-start(bf16[64,24,128]{2,1,0:T(8,128)(2,1)} %shard_map.129), calls=%async_computation.4 | async-start | bytes 786432 | tf_op jit(solution)/shard_map/all_to_all | solution.py:703
  128.8 5.7 %shard_map.131 = (f32[768,128]{1,0:T(8,128)}, f32[768,128]{1,0:T(8,128)}, f32[64,128]{1,0:T(8,128)}) custom-call(f32[1,768]{1,0:T(1,128)} %weights.3, f32[16,768]{1,0:T(8,128)} %get-tuple-element.59.side_p.refs_1_, bf16[768,128]{1,0:T(8,128)(2,1)} %get-tuple-element.91.near.refs_2_, bf16[768,128]{1,0:T(8,128)(2,1)} %get-tuple-element.92.refs_3_, ...), custom_call_target="tpu_custom_call" | custom-call | flops 603979776 | bytes 13655040 | tf_op jit(solution)/shard_map/pallas_call | solution.py:572
  134.5 4.3 %all-to-all-done.4.every = bf16[64,24,128]{2,1,0:T(8,128)(2,1)} async-done(((bf16[64,24,128]{2,1,0:T(8,128)(2,1)}), bf16[64,24,128]{2,1,0:T(8,128)(2,1)}, u32[]{:S(2)}, u32[]{:S(2)}) %all-to-all-start.4) | async-done | bytes 393248 | tf_op jit(solution)/shard_map/all_to_all | solution.py:703
  138.8 2.1 %shard_map.132 = (bf16[128,128]{1,0:T(8,128)(2,1)}, f32[128,2,128]{2,1,0:T(2,128)}) custom-call(bf16[64,24,128]{2,1,0:T(8,128)(2,1)} %all-to-all-done.4.every, bf16[48,1536]{1,0:T(8,128)(2,1)} %get-tuple-element.63.coarse, bf16[48,128]{1,0:T(8,128)(2,1)} %get-tuple-element.64.forms, f32[64,128]{1,0:T(8,128)} %get-tuple-element.93.stats), custom_call_target="tpu_custom_call" | custom-call | flops 18874368 | bytes 749568 | tf_op jit(solution)/shard_map/pallas_call | solution.py:572
  141.0 6.5 %all-to-all-start.5 = ((f32[128,2,128]{2,1,0:T(2,128)}), f32[128,2,128]{2,1,0:T(2,128)}, u32[]{:S(2)}, u32[]{:S(2)}) async-start(f32[128,2,128]{2,1,0:T(2,128)} %get-tuple-element.94), calls=%async_computation.5 | async-start | bytes 262144 | tf_op jit(solution)/shard_map/all_to_all | solution.py:745
  147.5 2.4 %shard_map.133 = (f32[768,128]{1,0:T(8,128)}, f32[768,128]{1,0:T(8,128)}) custom-call(bf16[128,128]{1,0:T(8,128)(2,1)} %get-tuple-element.96.stack, f32[768,128]{1,0:T(8,128)} %get-tuple-element.97.g, f32[768,128]{1,0:T(8,128)} %get-tuple-element.98.gp, bf16[768,128]{1,0:T(8,128)(2,1)} %get-tuple-element.57.md, bf16[768,128]{1,0:T(8,128)(2,1)} %get-tuple-element.75.md_p), custom_call_target="tpu_custom_call" | custom-call | flops 50331648 | bytes 1998848 | tf_op jit(solution)/shard_map/pallas_call | solution.py:572
  149.9 7.5 %all-to-all-done.5.refs_2_ = f32[128,2,128]{2,1,0:T(2,128)} async-done(((f32[128,2,128]{2,1,0:T(2,128)}), f32[128,2,128]{2,1,0:T(2,128)}, u32[]{:S(2)}, u32[]{:S(2)}) %all-to-all-start.5) | async-done | bytes 131104 | tf_op jit(solution)/shard_map/all_to_all | solution.py:745
  157.4 4.2 %shard_map.134 = (f32[768,128]{1,0:T(8,128)}, bf16[768,128]{1,0:T(8,128)(2,1)}, bf16[768,128]{1,0:T(8,128)(2,1)}, bf16[768,128]{1,0:T(8,128)(2,1)}, f32[24,128]{1,0:T(8,128)}) custom-call(f32[1,768]{1,0:T(1,128)} %weights.3, f32[8,768]{1,0:T(8,128)} %get-tuple-element.61.refs_1_, f32[128,2,128]{2,1,0:T(2,128)} %all-to-all-done.5.refs_2_, ...), custom_call_target="tpu_custom_call" | custom-call | flops 603979776 | bytes 15260672 | tf_op jit(solution)/shard_map/pallas_call | solution.py:572
  162.1 4.4 %shard_map.135.slave = f32[768,128]{1,0:T(8,128)} custom-call(bf16[768,128]{1,0:T(8,128)(2,1)} %get-tuple-element.103.load_m, bf16[768,128]{1,0:T(8,128)(2,1)} %get-tuple-element.104.load_s, f32[1,768]{1,0:T(1,128)} %weights.3, f32[1536,128]{1,0:T(8,128)} %shard_map.114.refs_7_.refs_9_.fixed, bf16[2304,2304]{1,0:T(8,128)(2,1)} %bitcast.15), custom_call_target="tpu_custom_call" | custom-call | flops 99999997952 | bytes 12192768 | tf_op jit(solution)/shard_map/pallas_call | solution.py:572
  167.1 2.2 %shard_map.136 = f32[768,128]{1,0:T(8,128)} custom-call(f32[768,128]{1,0:T(8,128)} %shard_map.135.slave, bf16[768,128]{1,0:T(8,128)(2,1)} %collective-permute-done.12.um_n, bf16[1152,128]{1,0:T(8,128)(2,1)} %get-tuple-element.68.refs_8_.tiles_s), custom_call_target="tpu_custom_call" | custom-call | flops 37748736 | bytes 1277952 | tf_op jit(solution)/shard_map/pallas_call | solution.py:572
  (30 shorter events, 14.7 us)
Async XLA Ops:
  3.4 9.1 %collective-permute-start = (bf16[1920,128]{1,0:T(8,128)(2,1)}, bf16[1920,128]{1,0:T(8,128)(2,1)}, u32[]{:S(2)}, u32[]{:S(2)}) collective-permute-start(bf16[1920,128]{1,0:T(8,128)(2,1)} %get-tuple-element.54.refs_4_), channel_id=1, source_target_pairs={{124,0},{0,4},{4,8},{8,12},{12,16},{16,20},{20,24},{24,28},{28,32}... | collective-permute-start | bytes 1474568 | tf_op jit(solution)/shard_map/ppermute | solution.py:22
  6.0 6.5 %collective-permute-start.1 = (f32[16,768]{1,0:T(8,128)}, f32[16,768]{1,0:T(8,128)}, u32[]{:S(2)}, u32[]{:S(2)}) collective-permute-start(f32[16,768]{1,0:T(8,128)} %get-tuple-element.55), channel_id=1, source_target_pairs={{4,0},{8,4},{12,8},{16,12},{20,16},{24,20},{28,24},{32,28},{36,32}... | collective-permute-start | bytes 147464 | tf_op jit(solution)/shard_map/ppermute | solution.py:22
  6.0 53.7 %collective-permute-start.5 = (f32[768,128]{1,0:T(8,128)}, f32[768,128]{1,0:T(8,128)}, u32[]{:S(2)}, u32[]{:S(2)}) collective-permute-start(f32[768,128]{1,0:T(8,128)} %bitcast.22), channel_id=1, source_target_pairs={{124,0},{0,4},{4,8},{8,12},{12,16},{16,20},{20,24},{24,28},{28,32}... | collective-permute-start | bytes 1179656 | tf_op jit(solution)/shard_map/ppermute | solution.py:22
  19.9 5.5 %collective-permute-start.2 = (f32[24,128]{1,0:T(8,128)}, f32[24,128]{1,0:T(8,128)}, u32[]{:S(2)}, u32[]{:S(2)}) collective-permute-start(f32[24,128]{1,0:T(8,128)} %get-tuple-element.62.resid), channel_id=1, source_target_pairs={{4,0},{0,4},{12,8},{8,12},{20,16},{16,20},{28,24},{24,28},{36,32},... | collective-permute-start | bytes 36872 | tf_op jit(solution)/shard_map/ppermute | solution.py:27
  24.8 15.4 %collective-permute-start.3 = (bf16[768,128]{1,0:T(8,128)(2,1)}, bf16[768,128]{1,0:T(8,128)(2,1)}, u32[]{:S(2)}, u32[]{:S(2)}) collective-permute-start(bf16[768,128]{1,0:T(8,128)(2,1)} %get-tuple-element.60.near.refs_2_), channel_id=1, source_target_pairs={{4,0},{0,4},{12,8},{8,12},{20,16},{16,20},{28,24},{24,28},{36,32},... | collective-permute-start | bytes 589832 | tf_op jit(solution)/shard_map/ppermute | solution.py:27
  24.8 15.4 %collective-permute-start.4 = (bf16[768,128]{1,0:T(8,128)(2,1)}, bf16[768,128]{1,0:T(8,128)(2,1)}, u32[]{:S(2)}, u32[]{:S(2)}) collective-permute-start(bf16[768,128]{1,0:T(8,128)(2,1)} %get-tuple-element.65.refs_3_), channel_id=1, source_target_pairs={{124,0},{8,4},{4,8},{16,12},{12,16},{24,20},{20,24},{32,28},{28,32... | collective-permute-start | bytes 589832 | tf_op jit(solution)/shard_map/ppermute | solution.py:33
  26.9 22.3 %all-to-all-start = ((bf16[64,24,128]{2,1,0:T(8,128)(2,1)}), bf16[64,24,128]{2,1,0:T(8,128)(2,1)}, u32[]{:S(2)}, u32[]{:S(2)}) async-start(bf16[64,24,128]{2,1,0:T(8,128)(2,1)} %shard_map.117), calls=%async_computation | async-start | bytes 786432 | tf_op jit(solution)/shard_map/all_to_all | solution.py:703
  51.3 15.8 %all-to-all-start.1 = ((f32[128,2,128]{2,1,0:T(2,128)}), f32[128,2,128]{2,1,0:T(2,128)}, u32[]{:S(2)}, u32[]{:S(2)}) async-start(f32[128,2,128]{2,1,0:T(2,128)} %get-tuple-element.71), calls=%async_computation.1 | async-start | bytes 262144 | tf_op jit(solution)/shard_map/all_to_all | solution.py:745
  72.6 2.4 %collective-permute-start.6 = (f32[24,128]{1,0:T(8,128)}, f32[24,128]{1,0:T(8,128)}, u32[]{:S(2)}, u32[]{:S(2)}) collective-permute-start(f32[24,128]{1,0:T(8,128)} %get-tuple-element.78.resid), channel_id=1, source_target_pairs={{4,0},{0,4},{12,8},{8,12},{20,16},{16,20},{28,24},{24,28},{36,32},... | collective-permute-start | bytes 36872 | tf_op jit(solution)/shard_map/ppermute | solution.py:27
  73.1 10.4 %collective-permute-start.8 = (bf16[768,128]{1,0:T(8,128)(2,1)}, bf16[768,128]{1,0:T(8,128)(2,1)}, u32[]{:S(2)}, u32[]{:S(2)}) collective-permute-start(bf16[768,128]{1,0:T(8,128)(2,1)} %get-tuple-element.80.refs_3_), channel_id=1, source_target_pairs={{124,0},{8,4},{4,8},{16,12},{12,16},{24,20},{20,24},{32,28},{28,32... | collective-permute-start | bytes 589832 | tf_op jit(solution)/shard_map/ppermute | solution.py:33
  73.4 10.1 %collective-permute-start.7 = (bf16[768,128]{1,0:T(8,128)(2,1)}, bf16[768,128]{1,0:T(8,128)(2,1)}, u32[]{:S(2)}, u32[]{:S(2)}) collective-permute-start(bf16[768,128]{1,0:T(8,128)(2,1)} %get-tuple-element.79.near.refs_2_), channel_id=1, source_target_pairs={{4,0},{0,4},{12,8},{8,12},{20,16},{16,20},{28,24},{24,28},{36,32},... | collective-permute-start | bytes 589832 | tf_op jit(solution)/shard_map/ppermute | solution.py:27
  76.6 17.0 %all-to-all-start.2 = ((bf16[64,24,128]{2,1,0:T(8,128)(2,1)}), bf16[64,24,128]{2,1,0:T(8,128)(2,1)}, u32[]{:S(2)}, u32[]{:S(2)}) async-start(bf16[64,24,128]{2,1,0:T(8,128)(2,1)} %shard_map.123), calls=%async_computation.2 | async-start | bytes 786432 | tf_op jit(solution)/shard_map/all_to_all | solution.py:703
  95.7 16.5 %all-to-all-start.3 = ((f32[128,2,128]{2,1,0:T(2,128)}), f32[128,2,128]{2,1,0:T(2,128)}, u32[]{:S(2)}, u32[]{:S(2)}) async-start(f32[128,2,128]{2,1,0:T(2,128)} %get-tuple-element.82), calls=%async_computation.3 | async-start | bytes 262144 | tf_op jit(solution)/shard_map/all_to_all | solution.py:745
  117.7 2.6 %collective-permute-start.9 = (f32[24,128]{1,0:T(8,128)}, f32[24,128]{1,0:T(8,128)}, u32[]{:S(2)}, u32[]{:S(2)}) collective-permute-start(f32[24,128]{1,0:T(8,128)} %get-tuple-element.90.resid), channel_id=1, source_target_pairs={{4,0},{0,4},{12,8},{8,12},{20,16},{16,20},{28,24},{24,28},{36,32},... | collective-permute-start | bytes 36872 | tf_op jit(solution)/shard_map/ppermute | solution.py:27
  118.2 10.6 %collective-permute-start.11 = (bf16[768,128]{1,0:T(8,128)(2,1)}, bf16[768,128]{1,0:T(8,128)(2,1)}, u32[]{:S(2)}, u32[]{:S(2)}) collective-permute-start(bf16[768,128]{1,0:T(8,128)(2,1)} %get-tuple-element.92.refs_3_), channel_id=1, source_target_pairs={{124,0},{8,4},{4,8},{16,12},{12,16},{24,20},{20,24},{32,28},{28,32... | collective-permute-start | bytes 589832 | tf_op jit(solution)/shard_map/ppermute | solution.py:33
  118.7 10.1 %collective-permute-start.10 = (bf16[768,128]{1,0:T(8,128)(2,1)}, bf16[768,128]{1,0:T(8,128)(2,1)}, u32[]{:S(2)}, u32[]{:S(2)}) collective-permute-start(bf16[768,128]{1,0:T(8,128)(2,1)} %get-tuple-element.91.near.refs_2_), channel_id=1, source_target_pairs={{4,0},{0,4},{12,8},{8,12},{20,16},{16,20},{28,24},{24,28},{36,32},... | collective-permute-start | bytes 589832 | tf_op jit(solution)/shard_map/ppermute | solution.py:27
  121.8 17.1 %all-to-all-start.4 = ((bf16[64,24,128]{2,1,0:T(8,128)(2,1)}), bf16[64,24,128]{2,1,0:T(8,128)(2,1)}, u32[]{:S(2)}, u32[]{:S(2)}) async-start(bf16[64,24,128]{2,1,0:T(8,128)(2,1)} %shard_map.129), calls=%async_computation.4 | async-start | bytes 786432 | tf_op jit(solution)/shard_map/all_to_all | solution.py:703
  141.0 16.5 %all-to-all-start.5 = ((f32[128,2,128]{2,1,0:T(2,128)}), f32[128,2,128]{2,1,0:T(2,128)}, u32[]{:S(2)}, u32[]{:S(2)}) async-start(f32[128,2,128]{2,1,0:T(2,128)} %get-tuple-element.94), calls=%async_computation.5 | async-start | bytes 262144 | tf_op jit(solution)/shard_map/all_to_all | solution.py:745
  161.7 5.5 %collective-permute-start.12 = (bf16[768,128]{1,0:T(8,128)(2,1)}, bf16[768,128]{1,0:T(8,128)(2,1)}, u32[]{:S(2)}, u32[]{:S(2)}) collective-permute-start(bf16[768,128]{1,0:T(8,128)(2,1)} %get-tuple-element.105), channel_id=1, source_target_pairs={{4,0},{8,4},{12,8},{16,12},{20,16},{24,20},{28,24},{32,28},{36,32}... | collective-permute-start | bytes 589832 | tf_op jit(solution)/shard_map/ppermute | solution.py:22
